TPU v7x, 256 devices: a whole 4x4x8 slice. The times are simulated.
256 devices in a mesh: dp: 32 (over z, x_lo, core), grp: 8 (over x_hi, y).
Axes of the slice: x: 4 (x_hi: 2, x_lo: 2; x = x_hi * 2 + x_lo), y: 4, z: 8, core: 2. Of those that a mesh axis runs over, the one named last changes fastest.
Arguments:
- acts: bfloat16 [8, 32768, 1024], P(None, ('dp', 'grp')), may hold values from -24 to 24
- grads: bfloat16 [8, 32768, 1024], P(None, ('dp', 'grp')), may hold values from -0.125 to 0.125
- assign: int32 [8], replicated, may hold values from 0 to 7, each once
- bases_a: bfloat16 [8, 1024, 1024], P('grp', 'dp'), may hold values from -0.1875 to 0.1875
- bases_g: bfloat16 [8, 1024, 1024], P('grp', 'dp'), may hold values from -0.1875 to 0.1875
- eig_a: float32 [8, 1024], P('grp'), may hold values from 0.3 to 2
- eig_g: float32 [8, 1024], P('grp'), may hold values from 0.3 to 2
Outputs:
- factor_a: float32 [8, 1024, 1024], P('grp', 'dp')
- factor_g: float32 [8, 1024, 1024], P('grp', 'dp')
- precond: bfloat16 [8, 1024, 1024], P(None, 'dp')
Inputs may be any that keep to these rules, and one draw needn't show every extreme that they name: assign is a permutation of the slots; slot k belongs to the owner group k // (8 / number of groups).
All inputs are finite; a program needn't handle non-finite values.
Results may differ from a plain program's by a relative error of at most 0.0085.
Values may be sent and summed in bfloat16 or wider, within the bound.
No kernel may reach another device: no remote copies, remote signals or barrier semaphores. Data moves between devices by JAX's collectives and lax.ppermute only.
A program may use at most 128 MiB of HBM per device.

v0:
```python
import jax
import jax.numpy as jnp
from jax import lax
from jax.experimental import pallas as pl
from jax.experimental.pallas import tpu as pltpu
from jax.sharding import Mesh, PartitionSpec as P

damping_term = 0.1
bf16, f32 = jnp.bfloat16, jnp.float32
GRP = ("xh", "y")
DP = ("z", "xl", "core")
contract_first = (((0,), (0,)), ((), ()))
contract_last = (((1,), (1,)), ((), ()))


def pick_kernel(assign, grads, acts, dst, buf, got, put):
    n = grads.shape[0]
    loads, stores = [], []
    for slot in range(n):
        owned = jnp.int32(0)
        for p in range(n):
            owned = owned + jnp.where(assign[p] == slot, p, 0)
        for i, src in enumerate((grads, acts)):
            loads.append(pltpu.make_async_copy(src.at[owned], buf.at[slot, i], got.at[slot, i]))
            stores.append(pltpu.make_async_copy(buf.at[slot, i], dst.at[slot, i], put.at[slot, i]))
    for load in loads:
        load.start()
    for load, store in zip(loads, stores):
        load.wait()
        store.start()
    for store in stores:
        store.wait()


def pick(assign, grads, acts):
    n, rows, width = grads.shape
    both = (n, 2, rows, width)
    return pl.pallas_call(
        pick_kernel,
        in_specs=[pl.BlockSpec(memory_space=pltpu.SMEM)] + [pl.BlockSpec(memory_space=pl.ANY)] * 2,
        out_specs=pl.BlockSpec(memory_space=pl.ANY),
        out_shape=jax.ShapeDtypeStruct(both, grads.dtype),
        scratch_shapes=[
            pltpu.VMEM(both, grads.dtype),
            pltpu.SemaphoreType.DMA((n, 2)),
            pltpu.SemaphoreType.DMA((n, 2)),
        ],
        cost_estimate=pl.CostEstimate(flops=0, bytes_accessed=8 * grads.size, transcendentals=0),
    )(assign, grads, acts)


def order_kernel(index, *refs):
    n = len(refs) - 4
    pieces, (out, buf, got, put) = refs[:n], refs[n:]
    loads = [pltpu.make_async_copy(pieces[s], buf.at[s], got.at[s]) for s in range(n)]
    for load in loads:
        load.start()
    for load in loads:
        load.wait()
    stores = [pltpu.make_async_copy(buf.at[index[j]], out.at[j], put.at[j]) for j in range(n)]
    for store in stores:
        store.start()
    for store in stores:
        store.wait()


def order(index, pieces):
    n = len(pieces)
    shape = (n,) + pieces[0].shape
    return pl.pallas_call(
        order_kernel,
        in_specs=[pl.BlockSpec(memory_space=pltpu.SMEM)] + [pl.BlockSpec(memory_space=pl.ANY)] * n,
        out_specs=pl.BlockSpec(memory_space=pl.ANY),
        out_shape=jax.ShapeDtypeStruct(shape, pieces[0].dtype),
        scratch_shapes=[
            pltpu.VMEM(shape, pieces[0].dtype),
            pltpu.SemaphoreType.DMA((n,)),
            pltpu.SemaphoreType.DMA((n,)),
        ],
    )(index, *pieces)


def weave_kernel(where, mine, other, out_g, out_a, buf, got, put):
    loads = [pltpu.make_async_copy(x, buf.at[i], got.at[i]) for i, x in enumerate((mine, other))]
    for load in loads:
        load.start()
    for load in loads:
        load.wait()
    stores = []
    for b, out in enumerate((out_g, out_a)):
        for c in range(2):
            held = lax.rem(where[0] + c, 2)
            stores.append(
                pltpu.make_async_copy(buf.at[held, :, b], out.at[:, :, c], put.at[2 * b + c])
            )
    for store in stores:
        store.start()
    for store in stores:
        store.wait()


def weave(core, mine, other):
    n_z, _, n_xl, rows, width = mine.shape
    whole = jax.ShapeDtypeStruct((n_z, n_xl, 2, rows, width), mine.dtype)
    return pl.pallas_call(
        weave_kernel,
        in_specs=[pl.BlockSpec(memory_space=pltpu.SMEM)] + [pl.BlockSpec(memory_space=pl.ANY)] * 2,
        out_specs=[pl.BlockSpec(memory_space=pl.ANY)] * 2,
        out_shape=[whole, whole],
        scratch_shapes=[
            pltpu.VMEM((2,) + mine.shape, mine.dtype),
            pltpu.SemaphoreType.DMA((2,)),
            pltpu.SemaphoreType.DMA((4,)),
        ],
        compiler_params=pltpu.CompilerParams(vmem_limit_bytes=32 << 20),
    )(core.reshape(1), mine, other)


def spread_sum_kernel(src, out):
    total = src[0].astype(jnp.float32)
    for i in range(1, src.shape[0]):
        total = total + src[i].astype(jnp.float32)
    total = total.astype(out.dtype)
    for i in range(out.shape[0]):
        out[i] = total


def spread_sum(parts, copies):
    return pl.pallas_call(
        spread_sum_kernel,
        in_specs=[pl.BlockSpec(memory_space=pltpu.VMEM)],
        out_specs=pl.BlockSpec(memory_space=pltpu.VMEM),
        out_shape=jax.ShapeDtypeStruct((copies,) + parts.shape[1:], parts.dtype),
        compiler_params=pltpu.CompilerParams(vmem_limit_bytes=16 << 20),
    )(parts)


def chain_kernel(rotated, basis, left, eig_rows, eig_cols, out):
    mixed = jnp.dot(rotated[...], basis[...], preferred_element_type=f32)
    scaled = (mixed / (eig_rows[...] * eig_cols[...] + damping_term)).astype(bf16)
    back = lax.dot_general(scaled, basis[...], contract_last, preferred_element_type=f32)
    out[...] = jnp.dot(left[...], back.astype(bf16), preferred_element_type=f32)


def chain(rotated, basis, left, eig_rows, eig_cols):
    return pl.pallas_call(
        chain_kernel,
        in_specs=[pl.BlockSpec(memory_space=pltpu.VMEM)] * 5,
        out_specs=pl.BlockSpec(memory_space=pltpu.VMEM),
        out_shape=jax.ShapeDtypeStruct((left.shape[0], basis.shape[0]), f32),
        compiler_params=pltpu.CompilerParams(vmem_limit_bytes=32 << 20),
    )(rotated, basis, left, eig_rows, eig_cols)


def body(acts, grads, assign, bases_a, bases_g, eig_a, eig_g):
    n_proj = acts.shape[0]
    width = acts.shape[2]
    n_z, n_xl, n_core = (lax.axis_size(a) for a in DP)
    n_grp = lax.axis_size("xh") * lax.axis_size("y")
    n_dp = n_z * n_xl * n_core
    rows = width // n_dp
    tokens = acts.shape[1] * n_dp * n_grp
    z, xl, core = (lax.axis_index(a) for a in DP)

    def swap(x, axis):
        return lax.ppermute(x, axis, [(0, 1), (1, 0)])

    def in_order(index, mine, other):
        return jnp.where(index == 0, mine, other), jnp.where(index == 0, other, mine)

    mine = jnp.stack([bases_g[0], bases_a[0]])
    other, send = lax.optimization_barrier((swap(mine, "xl"), pick(assign, grads, acts)))
    mine = jnp.stack(in_order(xl, mine, other), axis=1)
    pieces = [mine] * n_z
    up = down = mine
    for s in range(1, n_z // 2 + 1):
        pieces[s] = up = lax.ppermute(up, "z", [(i, (i + 1) % n_z) for i in range(n_z)])
        if s < n_z // 2:
            pieces[-s] = down = lax.ppermute(down, "z", [(i, (i - 1) % n_z) for i in range(n_z)])
    mine = order(lax.rem(z - jnp.arange(n_z, dtype=jnp.int32) + n_z, n_z), pieces)
    full_g, full_a = (x.reshape(width, width) for x in weave(core, mine, swap(mine, "core")))

    own = lax.all_to_all(send, GRP, 0, 0, tiled=True)
    own, full_g, full_a = lax.optimization_barrier((own, full_g, full_a))
    own_g = own[:, 0].reshape(-1, width)
    own_a = own[:, 1].reshape(-1, width)

    def dot_first(x, y):
        return lax.dot_general(x, y, contract_first, preferred_element_type=f32)

    def half_sum(parts, axis, index, dim):
        keep = lax.dynamic_index_in_dim(parts, index, dim, False)
        give = lax.dynamic_index_in_dim(parts, 1 - index, dim, False)
        return (keep.astype(f32) + swap(give.astype(bf16), axis).astype(f32)).astype(bf16)

    def core_sum(total):
        return half_sum(total.reshape(n_z, n_xl, n_core, rows, width), "core", core, 2)

    turned = jnp.dot(own_g, full_g, preferred_element_type=f32).astype(bf16)
    half = width // n_core
    give = lax.dynamic_slice_in_dim(turned, (1 - core) * half, half, 1)
    keep = lax.dynamic_slice_in_dim(turned, core * half, half, 1)
    give = swap(dot_first(give, own_a).astype(bf16), "core")
    kept = lax.optimization_barrier(dot_first(keep, own_a).astype(bf16))
    pair = (kept.astype(f32) + give.astype(f32)).astype(bf16)
    pair = pair.reshape(n_xl * n_z, rows, width)
    own_g, own_a, pair = lax.optimization_barrier((own_g, own_a, pair))
    half_g = core_sum(dot_first(own_g, own_g))
    half_a = core_sum(dot_first(own_a, own_a) / tokens)
    halves = half_sum(jnp.concatenate([half_g, half_a], axis=2), "xl", xl, 1)
    spread = spread_sum(lax.all_to_all(pair, ("xl", "z"), 0, 0, tiled=True), n_z)
    rotated = lax.all_to_all(spread, "z", 0, 0, tiled=True).reshape(n_z * rows, width)

    quarter = n_z * rows
    first = (core * n_xl + xl) * quarter
    eig_rows = lax.dynamic_slice_in_dim(eig_g[0], first, quarter, 0)
    family = n_xl * n_core * rows
    left = lax.dynamic_slice(full_g, (z * family, first), (family, quarter))
    left = left.reshape(n_xl, n_core, rows, quarter).swapaxes(0, 1).reshape(family, quarter)
    result = chain(rotated, full_a, left, eig_rows[:, None], eig_a)

    def fold(x, axis, index):
        halves = x.reshape(2, -1, width)
        keep = lax.dynamic_index_in_dim(halves, index, 0, False)
        give = lax.dynamic_index_in_dim(halves, 1 - index, 0, False)
        return keep + swap(give, axis)

    result = fold(result, "core", core)
    halves, result = lax.optimization_barrier((halves, result))
    sums = jnp.sum(lax.all_to_all(halves, "z", 0, 0, tiled=True).astype(f32), axis=0)
    factor_g, factor_a = sums[:rows], sums[rows:]
    result = fold(result, "xl", xl).astype(bf16)
    pieces = [result]
    for s in range(1, n_grp):
        pieces.append(lax.ppermute(result, GRP, [(i, (i + s) % n_grp) for i in range(n_grp)]))
    me = lax.axis_index(GRP)
    index = lax.rem(me - assign + n_grp, n_grp)[:, None, None]
    precond = jnp.broadcast_to(pieces[0][None], (n_proj, rows, width))
    for s in range(1, n_grp):
        precond = jnp.where(index == s, pieces[s][None], precond)
    return (factor_a[None], factor_g[None], precond)


def solution(mesh):
    cut = Mesh(mesh.devices.reshape(8, 2, 2, 2, 4), DP + GRP)
    in_specs = (
        P(None, DP + GRP, None),
        P(None, DP + GRP, None),
        P(),
        P(GRP, DP, None),
        P(GRP, DP, None),
        P(GRP, None),
        P(GRP, None),
    )
    out_specs = (P(GRP, DP, None), P(GRP, DP, None), P(None, DP, None))
    return jax.shard_map(body, mesh=cut, in_specs=in_specs, out_specs=out_specs, check_vma=False)
```

profile of v0, /device:TPU:1, one launch (start us, length us, event | category | flops | bytes accessed | tf_op | source)
XLA Modules:
  0.0 174.3 jit_solution(4623126560108602819)
XLA Ops:
  2.3 2.0 %collective-permute-start = (bf16[2,32,1024]{2,1,0:T(8,128)(2,1)S(1)}, bf16[2,32,1024]{2,1,0:T(8,128)(2,1)S(1)}, u32[]{:S(2)}, u32[]{:S(2)}) collective-permute-start(bf16[2,32,1024]{2,1,0:T(8,128)(2,1)S(1)} %constant_dynamic-update-slice_fusion), channel_id=1, source_target_pairs={{0,16},{16,0},{1,17},{17,1},{2,18},{18,2},{3,19},{19,3},{4,20},{20... | collective-permute-start | bytes 393224 | tf_op jit(solution)/shard_map/ppermute | solution.py:166
  4.4 4.6 %shard_map.94 = bf16[8,2,128,1024]{3,2,1,0:T(8,128)(2,1)} custom-call(s32[8]{0:T(128)} %assign.1, bf16[8,128,1024]{2,1,0:T(8,128)(2,1)} %grads.1, bf16[8,128,1024]{2,1,0:T(8,128)(2,1)} %acts.1), custom_call_target="tpu_custom_call" | custom-call | bytes 8388608 | tf_op jit(solution)/shard_map/pallas_call | solution.py:38
  9.0 6.4 %all-to-all-start = ((bf16[8,2,128,1024]{3,2,1,0:T(8,128)(2,1)}), bf16[8,2,128,1024]{3,2,1,0:T(8,128)(2,1)}, u32[]{:S(2)}, u32[]{:S(2)}) async-start(bf16[8,2,128,1024]{3,2,1,0:T(8,128)(2,1)} %shard_map.94), calls=%async_computation | async-start | bytes 8388608 | tf_op jit(solution)/shard_map/all_to_all | solution.py:183
  15.4 1.7 collective-permute-start.1
  17.1 4.0 %collective-permute-start.5 = (bf16[2,2,32,1024]{3,2,1,0:T(8,128)(2,1)S(1)}, bf16[2,2,32,1024]{3,2,1,0:T(8,128)(2,1)S(1)}, u32[]{:S(2)}, u32[]{:S(2)}) collective-permute-start(bf16[2,2,32,1024]{3,2,1,0:T(8,128)(2,1)S(1)} %pad_maximum_fusion.refs_0_), channel_id=1, source_target_pairs={{0,224},{32,0},{64,32},{96,64},{128,96},{160,128},{192,160},{224,1... | collective-permute-start | bytes 786440 | tf_op jit(solution)/shard_map/ppermute | solution.py:179
  21.1 5.4 %collective-permute-done.1.refs_1_ = bf16[2,2,32,1024]{3,2,1,0:T(8,128)(2,1)S(1)} collective-permute-done((bf16[2,2,32,1024]{3,2,1,0:T(8,128)(2,1)S(1)}, bf16[2,2,32,1024]{3,2,1,0:T(8,128)(2,1)S(1)}, u32[]{:S(2)}, u32[]{:S(2)}) %collective-permute-start.1) | collective-permute-done | bytes 262176 | tf_op jit(solution)/shard_map/ppermute | solution.py:177
  26.6 2.7 %collective-permute-start.6 = (bf16[2,2,32,1024]{3,2,1,0:T(8,128)(2,1)S(1)}, bf16[2,2,32,1024]{3,2,1,0:T(8,128)(2,1)S(1)}, u32[]{:S(2)}, u32[]{:S(2)}) collective-permute-start(bf16[2,2,32,1024]{3,2,1,0:T(8,128)(2,1)S(1)} %collective-permute-done.5.refs_7_), channel_id=1, source_target_pairs={{0,224},{32,0},{64,32},{96,64},{128,96},{160,128},{192,160},{224,1... | collective-permute-start | bytes 786440 | tf_op jit(solution)/shard_map/ppermute | solution.py:179
  29.2 4.7 %collective-permute-done.2.refs_2_ = bf16[2,2,32,1024]{3,2,1,0:T(8,128)(2,1)S(1)} collective-permute-done((bf16[2,2,32,1024]{3,2,1,0:T(8,128)(2,1)S(1)}, bf16[2,2,32,1024]{3,2,1,0:T(8,128)(2,1)S(1)}, u32[]{:S(2)}, u32[]{:S(2)}) %collective-permute-start.2) | collective-permute-done | bytes 262176 | tf_op jit(solution)/shard_map/ppermute | solution.py:177
  33.9 2.7 %collective-permute-start.7 = (bf16[2,2,32,1024]{3,2,1,0:T(8,128)(2,1)S(1)}, bf16[2,2,32,1024]{3,2,1,0:T(8,128)(2,1)S(1)}, u32[]{:S(2)}, u32[]{:S(2)}) collective-permute-start(bf16[2,2,32,1024]{3,2,1,0:T(8,128)(2,1)S(1)} %collective-permute-done.6.refs_6_), channel_id=1, source_target_pairs={{0,224},{32,0},{64,32},{96,64},{128,96},{160,128},{192,160},{224,1... | collective-permute-start | bytes 786440 | tf_op jit(solution)/shard_map/ppermute | solution.py:179
  36.6 4.2 %collective-permute-done.3.refs_3_ = bf16[2,2,32,1024]{3,2,1,0:T(8,128)(2,1)S(1)} collective-permute-done((bf16[2,2,32,1024]{3,2,1,0:T(8,128)(2,1)S(1)}, bf16[2,2,32,1024]{3,2,1,0:T(8,128)(2,1)S(1)}, u32[]{:S(2)}, u32[]{:S(2)}) %collective-permute-start.3) | collective-permute-done | bytes 262176 | tf_op jit(solution)/shard_map/ppermute | solution.py:177
  41.3 6.3 %collective-permute-done.4.refs_4_ = bf16[2,2,32,1024]{3,2,1,0:T(8,128)(2,1)S(1)} collective-permute-done((bf16[2,2,32,1024]{3,2,1,0:T(8,128)(2,1)S(1)}, bf16[2,2,32,1024]{3,2,1,0:T(8,128)(2,1)S(1)}, u32[]{:S(2)}, u32[]{:S(2)}) %collective-permute-start.4) | collective-permute-done | bytes 262176 | tf_op jit(solution)/shard_map/ppermute | solution.py:177
  48.3 3.6 %shard_map.95.mine = bf16[8,2,2,32,1024]{4,3,2,1,0:T(8,128)(2,1)} custom-call(s32[8]{0:T(128)} %compare_select_fusion.2.index, bf16[2,2,32,1024]{3,2,1,0:T(8,128)(2,1)} %copy-done.19, bf16[2,2,32,1024]{3,2,1,0:T(8,128)(2,1)} %copy-done.20, bf16[2,2,32,1024]{3,2,1,0:T(8,128)(2,1)} %copy-done.22, bf16[2,2,32,1024]{3,2,1,0:T(8,128)(2,1)} %copy-done.24, ...), custom_call_target="tpu_custom_call" | custom-call | tf_op jit(solution)/shard_map/pallas_call | solution.py:70
  52.0 4.2 %collective-permute-start.8 = (bf16[8,2,2,32,1024]{4,3,2,1,0:T(8,128)(2,1)}, bf16[8,2,2,32,1024]{4,3,2,1,0:T(8,128)(2,1)S(1)}, u32[]{:S(2)}, u32[]{:S(2)}) collective-permute-start(bf16[8,2,2,32,1024]{4,3,2,1,0:T(8,128)(2,1)} %shard_map.95.mine), channel_id=1, source_target_pairs={{0,8},{8,0},{1,9},{9,1},{2,10},{10,2},{3,11},{11,3},{4,12},{12,4},... | collective-permute-start | bytes 6291464 | tf_op jit(solution)/shard_map/ppermute | solution.py:166
  56.1 4.0 %collective-permute-done.8.other = bf16[8,2,2,32,1024]{4,3,2,1,0:T(8,128)(2,1)S(1)} collective-permute-done((bf16[8,2,2,32,1024]{4,3,2,1,0:T(8,128)(2,1)}, bf16[8,2,2,32,1024]{4,3,2,1,0:T(8,128)(2,1)S(1)}, u32[]{:S(2)}, u32[]{:S(2)}) %collective-permute-start.8) | collective-permute-done | bytes 2097184 | tf_op jit(solution)/shard_map/ppermute | solution.py:166
  60.1 1.4 copy-done.3
  61.5 1.6 copy-done.1
  63.1 1.6 copy-done.4
  65.4 1.3 copy-done.6
  66.7 2.8 %fusion.17 = (bf16[8,1,128,1024]{3,2,1,0:T(8,128)(2,1)S(1)}, bf16[8,1,128,1024]{3,2,1,0:T(8,128)(2,1)S(1)}) fusion(bf16[8,2,128,1024]{3,2,1,0:T(8,128)(2,1)} %all-to-all-done), kind=kLoop, calls=%fused_computation.56 | loop fusion | bytes 8388608 | tf_op jit(solution)/shard_map/slice | solution.py:186
  69.5 2.3 %convolution_convert_fusion = bf16[1024,1024]{1,0:T(8,128)(2,1)S(1)} fusion(bf16[1024,1024]{1,0:T(8,128)(2,1)S(1)} %bitcast.83, bf16[1024,1024]{1,0:T(8,128)(2,1)S(1)} %bitcast.74), kind=kOutput, calls=%fused_computation.15 | convolution fusion | flops 2148532224 | bytes 6291456 | tf_op jit(solution)/shard_map/dot_general | solution.py:199
  71.9 1.3 convolution_convert_fusion.1
  73.9 3.2 %convolution_convert_fusion.2 = bf16[512,1024]{1,0:T(8,128)(2,1)S(1)} fusion(bf16[1024,1024]{1,0:T(8,128)(2,1)} %bitcast.76, bf16[1024,1024]{1,0:T(8,128)(2,1)} %copy-done.16, s32[]{:T(128)S(6)} %select_n.72), kind=kOutput, calls=%fused_computation.17 | convolution fusion | flops 1074266112 | bytes 4194308 | tf_op jit(solution)/shard_map/dot_general | solution.py:189
  77.1 2.5 %add_convert_fusion = bf16[512,1024]{1,0:T(8,128)(2,1)} fusion(bf16[512,1024]{1,0:T(8,128)(2,1)} %collective-permute-done.9, bf16[512,1024]{1,0:T(8,128)(2,1)S(1)} %convolution_convert_fusion.2), kind=kLoop, calls=%fused_computation.14 | loop fusion | flops 2097152 | bytes 3145728 | tf_op jit(solution)/shard_map/convert_element_type | solution.py:205
  79.6 6.5 %all-to-all-start.1 = ((bf16[16,32,1024]{2,1,0:T(8,128)(2,1)}), bf16[16,32,1024]{2,1,0:T(8,128)(2,1)S(1)}, u32[]{:S(2)}, u32[]{:S(2)}) async-start(bf16[16,32,1024]{2,1,0:T(8,128)(2,1)} %bitcast.78), calls=%async_computation.1 | async-start | bytes 2097152 | tf_op jit(solution)/shard_map/all_to_all | solution.py:211
  86.1 4.6 %convolution_multiply_fusion = f32[1024,1024]{1,0:T(8,128)S(1)} fusion(bf16[1024,1024]{1,0:T(8,128)(2,1)} %bitcast.77), kind=kOutput, calls=%fused_computation.4 | convolution fusion | flops 2148532224 | bytes 6291456 | tf_op jit(solution)/shard_map/dot_general | solution.py:189
  92.2 1.6 copy-done.18
  93.9 2.4 %fusion.18 = f32[1024,1024]{1,0:T(8,128)S(1)} fusion(bf16[1024,1024]{1,0:T(8,128)(2,1)S(1)} %bitcast.84), kind=kOutput, calls=%fused_computation.57 | convolution fusion | flops 2147483648 | bytes 6291456 | tf_op jit(solution)/shard_map/dot_general | solution.py:189
  96.3 2.0 %copy-done.14 = f32[1024,1024]{1,0:T(8,128)} copy-done((f32[1024,1024]{1,0:T(8,128)}, f32[1024,1024]{1,0:T(8,128)S(1)}, u32[]{:S(2)}) %copy-start.14) | copy-done | bytes 4194328
  99.7 2.4 %fusion.1 = bf16[8,2,32,1024]{3,2,1,0:T(8,128)(2,1)S(1)} fusion(bf16[8,2,32,1024]{3,2,1,0:T(8,128)(2,1)} %collective-permute-done.11, f32[8,2,2,32,1024]{4,3,2,1,0:T(8,128)} %bitcast.80, s32[]{:T(128)S(6)} %select_n.74), kind=kLoop, calls=%fused_computation.9 | loop fusion | flops 1572864 | bytes 4194308 | tf_op jit(solution)/shard_map/convert_element_type | solution.py:194
  102.8 1.6 fusion.2
  104.5 1.2 fusion.6
  105.8 1.6 collective-permute-start.12
  107.5 3.9 %all-to-all-done.1.src = bf16[16,32,1024]{2,1,0:T(8,128)(2,1)S(1)} async-done(((bf16[16,32,1024]{2,1,0:T(8,128)(2,1)}), bf16[16,32,1024]{2,1,0:T(8,128)(2,1)S(1)}, u32[]{:S(2)}, u32[]{:S(2)}) %all-to-all-start.1) | async-done | bytes 1048608 | tf_op jit(solution)/shard_map/all_to_all | solution.py:211
  112.3 5.5 %all-to-all-start.2 = ((bf16[8,32,1024]{2,1,0:T(8,128)(2,1)}), bf16[8,32,1024]{2,1,0:T(8,128)(2,1)S(1)}, u32[]{:S(2)}, u32[]{:S(2)}) async-start(bf16[8,32,1024]{2,1,0:T(8,128)(2,1)} %copy-done.2), calls=%async_computation.2 | async-start | bytes 1048576 | tf_op jit(solution)/shard_map/all_to_all | solution.py:212
  118.9 16.9 %all-to-all-done.2 = bf16[8,32,1024]{2,1,0:T(8,128)(2,1)S(1)} async-done(((bf16[8,32,1024]{2,1,0:T(8,128)(2,1)}), bf16[8,32,1024]{2,1,0:T(8,128)(2,1)S(1)}, u32[]{:S(2)}, u32[]{:S(2)}) %all-to-all-start.2) | async-done | bytes 524320 | tf_op jit(solution)/shard_map/all_to_all | solution.py:212
  135.8 1.4 shard_map.98
  137.9 2.7 %fusion = bf16[8,64,1024]{2,1,0:T(8,128)(2,1)} fusion(bf16[8,64,1024]{2,1,0:T(8,128)(2,1)} %collective-permute-done.12, s32[]{:T(128)S(6)} %select_n.76, bf16[8,2,32,1024]{3,2,1,0:T(8,128)(2,1)S(1)} %copy-done.12, bf16[8,2,32,1024]{3,2,1,0:T(8,128)(2,1)S(1)} %copy-done.10), kind=kLoop, calls=%fused_computation.7 | loop fusion | flops 4194304 | bytes 4194308 | tf_op jit(solution)/shard_map/convert_element_type | solution.py:194
  140.6 3.6 %all-to-all-start.3 = ((bf16[8,64,1024]{2,1,0:T(8,128)(2,1)}), bf16[8,64,1024]{2,1,0:T(8,128)(2,1)S(1)}, u32[]{:S(2)}, u32[]{:S(2)}) async-start(bf16[8,64,1024]{2,1,0:T(8,128)(2,1)} %fusion), calls=%async_computation.3 | async-start | bytes 2097152 | tf_op jit(solution)/shard_map/all_to_all | solution.py:230
  144.2 1.3 collective-permute-start.14
  145.5 3.9 %collective-permute-done.14 = f32[32,1024]{1,0:T(8,128)S(1)} collective-permute-done((f32[32,1024]{1,0:T(8,128)S(1)}, f32[32,1024]{1,0:T(8,128)S(1)}, u32[]{:S(2)}, u32[]{:S(2)}) %collective-permute-start.14) | collective-permute-done | bytes 131104 | tf_op jit(solution)/shard_map/ppermute | solution.py:166
  149.4 3.9 %collective-permute-start.15 = (bf16[32,1024]{1,0:T(8,128)(2,1)S(1)}, bf16[32,1024]{1,0:T(8,128)(2,1)S(1)}, u32[]{:S(2)}, u32[]{:S(2)}) collective-permute-start(bf16[32,1024]{1,0:T(8,128)(2,1)S(1)} %fusion.11), channel_id=1, source_target_pairs={{0,7},{1,0},{2,1},{3,2},{4,3},{5,4},{6,5},{7,6},{8,15},{9,8},{10,9... | collective-permute-start | bytes 196616 | tf_op jit(solution)/shard_map/ppermute | solution.py:235
  154.4 1.4 collective-permute-start.17
  155.8 1.5 collective-permute-start.18
  158.2 3.9 %collective-permute-start.20 = (bf16[32,1024]{1,0:T(8,128)(2,1)S(1)}, bf16[32,1024]{1,0:T(8,128)(2,1)S(1)}, u32[]{:S(2)}, u32[]{:S(2)}) collective-permute-start(bf16[32,1024]{1,0:T(8,128)(2,1)S(1)} %fusion.11), channel_id=1, source_target_pairs={{0,2},{1,3},{2,4},{3,5},{4,6},{5,7},{6,0},{7,1},{8,10},{9,11},{10,... | collective-permute-start | bytes 196616 | tf_op jit(solution)/shard_map/ppermute | solution.py:235
  162.1 1.2 collective-permute-done.19
  163.3 2.0 %collective-permute-done.20 = bf16[32,1024]{1,0:T(8,128)(2,1)S(1)} collective-permute-done((bf16[32,1024]{1,0:T(8,128)(2,1)S(1)}, bf16[32,1024]{1,0:T(8,128)(2,1)S(1)}, u32[]{:S(2)}, u32[]{:S(2)}) %collective-permute-start.20) | collective-permute-done | bytes 65568 | tf_op jit(solution)/shard_map/ppermute | solution.py:235
  165.3 4.1 %collective-permute-done.21 = bf16[32,1024]{1,0:T(8,128)(2,1)S(1)} collective-permute-done((bf16[32,1024]{1,0:T(8,128)(2,1)S(1)}, bf16[32,1024]{1,0:T(8,128)(2,1)S(1)}, u32[]{:S(2)}, u32[]{:S(2)}) %collective-permute-start.21) | collective-permute-done | bytes 65568 | tf_op jit(solution)/shard_map/ppermute | solution.py:235
  170.6 2.8 %all-to-all-done.3 = bf16[8,64,1024]{2,1,0:T(8,128)(2,1)S(1)} async-done(((bf16[8,64,1024]{2,1,0:T(8,128)(2,1)}), bf16[8,64,1024]{2,1,0:T(8,128)(2,1)S(1)}, u32[]{:S(2)}, u32[]{:S(2)}) %all-to-all-start.3) | async-done | bytes 1048608 | tf_op jit(solution)/shard_map/all_to_all | solution.py:230
  (96 shorter events, 14.8 us)
Async XLA Ops:
  0.6 117.2 %copy-start = (f32[1,1024]{1,0:T(1,128)S(1)}, f32[1,1024]{1,0:T(1,128)}, u32[]{:S(2)}) copy-start(f32[1,1024]{1,0:T(1,128)} %param.13) | copy-start | bytes 12292
  2.3 6.6 %collective-permute-start = (bf16[2,32,1024]{2,1,0:T(8,128)(2,1)S(1)}, bf16[2,32,1024]{2,1,0:T(8,128)(2,1)S(1)}, u32[]{:S(2)}, u32[]{:S(2)}) collective-permute-start(bf16[2,32,1024]{2,1,0:T(8,128)(2,1)S(1)} %constant_dynamic-update-slice_fusion), channel_id=1, source_target_pairs={{0,16},{16,0},{1,17},{17,1},{2,18},{18,2},{3,19},{19,3},{4,20},{20... | collective-permute-start | bytes 393224 | tf_op jit(solution)/shard_map/ppermute | solution.py:166
  9.0 57.7 %all-to-all-start = ((bf16[8,2,128,1024]{3,2,1,0:T(8,128)(2,1)}), bf16[8,2,128,1024]{3,2,1,0:T(8,128)(2,1)}, u32[]{:S(2)}, u32[]{:S(2)}) async-start(bf16[8,2,128,1024]{3,2,1,0:T(8,128)(2,1)} %shard_map.94), calls=%async_computation | async-start | bytes 8388608 | tf_op jit(solution)/shard_map/all_to_all | solution.py:183
  15.4 32.2 %copy-start.19 = (bf16[2,2,32,1024]{3,2,1,0:T(8,128)(2,1)}, bf16[2,2,32,1024]{3,2,1,0:T(8,128)(2,1)S(1)}, u32[]{:S(2)}) copy-start(bf16[2,2,32,1024]{3,2,1,0:T(8,128)(2,1)S(1)} %pad_maximum_fusion.refs_0_) | copy-start | bytes 786436
  15.4 11.2 %collective-permute-start.1 = (bf16[2,2,32,1024]{3,2,1,0:T(8,128)(2,1)S(1)}, bf16[2,2,32,1024]{3,2,1,0:T(8,128)(2,1)S(1)}, u32[]{:S(2)}, u32[]{:S(2)}) collective-permute-start(bf16[2,2,32,1024]{3,2,1,0:T(8,128)(2,1)S(1)} %pad_maximum_fusion.refs_0_), channel_id=1, source_target_pairs={{0,32},{32,64},{64,96},{96,128},{128,160},{160,192},{192,224},{224... | collective-permute-start | bytes 786440 | tf_op jit(solution)/shard_map/ppermute | solution.py:177
  17.1 9.4 %collective-permute-start.5 = (bf16[2,2,32,1024]{3,2,1,0:T(8,128)(2,1)S(1)}, bf16[2,2,32,1024]{3,2,1,0:T(8,128)(2,1)S(1)}, u32[]{:S(2)}, u32[]{:S(2)}) collective-permute-start(bf16[2,2,32,1024]{3,2,1,0:T(8,128)(2,1)S(1)} %pad_maximum_fusion.refs_0_), channel_id=1, source_target_pairs={{0,224},{32,0},{64,32},{96,64},{128,96},{160,128},{192,160},{224,1... | collective-permute-start | bytes 786440 | tf_op jit(solution)/shard_map/ppermute | solution.py:179
  26.6 21.0 %copy-start.20 = (bf16[2,2,32,1024]{3,2,1,0:T(8,128)(2,1)}, bf16[2,2,32,1024]{3,2,1,0:T(8,128)(2,1)S(1)}, u32[]{:S(2)}) copy-start(bf16[2,2,32,1024]{3,2,1,0:T(8,128)(2,1)S(1)} %collective-permute-done.1.refs_1_) | copy-start | bytes 786436
  26.6 7.4 %collective-permute-start.2 = (bf16[2,2,32,1024]{3,2,1,0:T(8,128)(2,1)S(1)}, bf16[2,2,32,1024]{3,2,1,0:T(8,128)(2,1)S(1)}, u32[]{:S(2)}, u32[]{:S(2)}) collective-permute-start(bf16[2,2,32,1024]{3,2,1,0:T(8,128)(2,1)S(1)} %collective-permute-done.1.refs_1_), channel_id=1, source_target_pairs={{0,32},{32,64},{64,96},{96,128},{128,160},{160,192},{192,224},{224... | collective-permute-start | bytes 786440 | tf_op jit(solution)/shard_map/ppermute | solution.py:177
  26.6 21.0 %copy-start.21 = (bf16[2,2,32,1024]{3,2,1,0:T(8,128)(2,1)}, bf16[2,2,32,1024]{3,2,1,0:T(8,128)(2,1)S(1)}, u32[]{:S(2)}) copy-start(bf16[2,2,32,1024]{3,2,1,0:T(8,128)(2,1)S(1)} %collective-permute-done.5.refs_7_) | copy-start | bytes 786436
  26.6 7.3 %collective-permute-start.6 = (bf16[2,2,32,1024]{3,2,1,0:T(8,128)(2,1)S(1)}, bf16[2,2,32,1024]{3,2,1,0:T(8,128)(2,1)S(1)}, u32[]{:S(2)}, u32[]{:S(2)}) collective-permute-start(bf16[2,2,32,1024]{3,2,1,0:T(8,128)(2,1)S(1)} %collective-permute-done.5.refs_7_), channel_id=1, source_target_pairs={{0,224},{32,0},{64,32},{96,64},{128,96},{160,128},{192,160},{224,1... | collective-permute-start | bytes 786440 | tf_op jit(solution)/shard_map/ppermute | solution.py:179
  33.9 13.7 %copy-start.22 = (bf16[2,2,32,1024]{3,2,1,0:T(8,128)(2,1)}, bf16[2,2,32,1024]{3,2,1,0:T(8,128)(2,1)S(1)}, u32[]{:S(2)}) copy-start(bf16[2,2,32,1024]{3,2,1,0:T(8,128)(2,1)S(1)} %collective-permute-done.2.refs_2_) | copy-start | bytes 786436
  33.9 6.8 %collective-permute-start.3 = (bf16[2,2,32,1024]{3,2,1,0:T(8,128)(2,1)S(1)}, bf16[2,2,32,1024]{3,2,1,0:T(8,128)(2,1)S(1)}, u32[]{:S(2)}, u32[]{:S(2)}) collective-permute-start(bf16[2,2,32,1024]{3,2,1,0:T(8,128)(2,1)S(1)} %collective-permute-done.2.refs_2_), channel_id=1, source_target_pairs={{0,32},{32,64},{64,96},{96,128},{128,160},{160,192},{192,224},{224... | collective-permute-start | bytes 786440 | tf_op jit(solution)/shard_map/ppermute | solution.py:177
  33.9 13.7 %copy-start.23 = (bf16[2,2,32,1024]{3,2,1,0:T(8,128)(2,1)}, bf16[2,2,32,1024]{3,2,1,0:T(8,128)(2,1)S(1)}, u32[]{:S(2)}) copy-start(bf16[2,2,32,1024]{3,2,1,0:T(8,128)(2,1)S(1)} %collective-permute-done.6.refs_6_) | copy-start | bytes 786436
  33.9 7.4 %collective-permute-start.7 = (bf16[2,2,32,1024]{3,2,1,0:T(8,128)(2,1)S(1)}, bf16[2,2,32,1024]{3,2,1,0:T(8,128)(2,1)S(1)}, u32[]{:S(2)}, u32[]{:S(2)}) collective-permute-start(bf16[2,2,32,1024]{3,2,1,0:T(8,128)(2,1)S(1)} %collective-permute-done.6.refs_6_), channel_id=1, source_target_pairs={{0,224},{32,0},{64,32},{96,64},{128,96},{160,128},{192,160},{224,1... | collective-permute-start | bytes 786440 | tf_op jit(solution)/shard_map/ppermute | solution.py:179
  40.7 6.9 %copy-start.24 = (bf16[2,2,32,1024]{3,2,1,0:T(8,128)(2,1)}, bf16[2,2,32,1024]{3,2,1,0:T(8,128)(2,1)S(1)}, u32[]{:S(2)}) copy-start(bf16[2,2,32,1024]{3,2,1,0:T(8,128)(2,1)S(1)} %collective-permute-done.3.refs_3_) | copy-start | bytes 786436
  40.7 6.8 %collective-permute-start.4 = (bf16[2,2,32,1024]{3,2,1,0:T(8,128)(2,1)S(1)}, bf16[2,2,32,1024]{3,2,1,0:T(8,128)(2,1)S(1)}, u32[]{:S(2)}, u32[]{:S(2)}) collective-permute-start(bf16[2,2,32,1024]{3,2,1,0:T(8,128)(2,1)S(1)} %collective-permute-done.3.refs_3_), channel_id=1, source_target_pairs={{0,32},{32,64},{64,96},{96,128},{128,160},{160,192},{192,224},{224... | collective-permute-start | bytes 786440 | tf_op jit(solution)/shard_map/ppermute | solution.py:177
  41.3 6.3 %copy-start.25 = (bf16[2,2,32,1024]{3,2,1,0:T(8,128)(2,1)}, bf16[2,2,32,1024]{3,2,1,0:T(8,128)(2,1)S(1)}, u32[]{:S(2)}) copy-start(bf16[2,2,32,1024]{3,2,1,0:T(8,128)(2,1)S(1)} %collective-permute-done.7.refs_5_) | copy-start | bytes 786436
  52.0 8.2 %collective-permute-start.8 = (bf16[8,2,2,32,1024]{4,3,2,1,0:T(8,128)(2,1)}, bf16[8,2,2,32,1024]{4,3,2,1,0:T(8,128)(2,1)S(1)}, u32[]{:S(2)}, u32[]{:S(2)}) collective-permute-start(bf16[8,2,2,32,1024]{4,3,2,1,0:T(8,128)(2,1)} %shard_map.95.mine), channel_id=1, source_target_pairs={{0,8},{8,0},{1,9},{9,1},{2,10},{10,2},{3,11},{11,3},{4,12},{12,4},... | collective-permute-start | bytes 6291464 | tf_op jit(solution)/shard_map/ppermute | solution.py:166
  61.5 1.6 copy-start.1
  63.1 1.6 copy-start.4
  66.7 2.9 %copy-start.7 = (bf16[8,2,2,32,1024]{4,3,2,1,0:T(8,128)(2,1)S(1)}, bf16[8,2,2,32,1024]{4,3,2,1,0:T(8,128)(2,1)}, u32[]{:S(2)}) copy-start(bf16[8,2,2,32,1024]{4,3,2,1,0:T(8,128)(2,1)} %copy-done.6) | copy-start | bytes 6291460
  69.5 2.4 %copy-start.17 = (bf16[8,1,128,1024]{3,2,1,0:T(8,128)(2,1)}, bf16[8,1,128,1024]{3,2,1,0:T(8,128)(2,1)S(1)}, u32[]{:S(2)}) copy-start(bf16[8,1,128,1024]{3,2,1,0:T(8,128)(2,1)S(1)} %get-tuple-element.30) | copy-start | bytes 6291460
  69.5 2.4 %copy-start.8 = (bf16[8,1,128,1024]{3,2,1,0:T(8,128)(2,1)}, bf16[8,1,128,1024]{3,2,1,0:T(8,128)(2,1)S(1)}, u32[]{:S(2)}) copy-start(bf16[8,1,128,1024]{3,2,1,0:T(8,128)(2,1)S(1)} %get-tuple-element.29) | copy-start | bytes 6291460
  73.2 3.8 %collective-permute-start.9 = (bf16[512,1024]{1,0:T(8,128)(2,1)S(1)}, bf16[512,1024]{1,0:T(8,128)(2,1)}, u32[]{:S(2)}, u32[]{:S(2)}) collective-permute-start(bf16[512,1024]{1,0:T(8,128)(2,1)S(1)} %convolution_convert_fusion.1), channel_id=1, source_target_pairs={{0,8},{8,0},{1,9},{9,1},{2,10},{10,2},{3,11},{11,3},{4,12},{12,4},... | collective-permute-start | bytes 3145736 | tf_op jit(solution)/shard_map/ppermute | solution.py:166
  79.6 31.8 %all-to-all-start.1 = ((bf16[16,32,1024]{2,1,0:T(8,128)(2,1)}), bf16[16,32,1024]{2,1,0:T(8,128)(2,1)S(1)}, u32[]{:S(2)}, u32[]{:S(2)}) async-start(bf16[16,32,1024]{2,1,0:T(8,128)(2,1)} %bitcast.78), calls=%async_computation.1 | async-start | bytes 2097152 | tf_op jit(solution)/shard_map/all_to_all | solution.py:211
  90.7 5.5 %copy-start.13 = (f32[1024,1024]{1,0:T(8,128)}, f32[1024,1024]{1,0:T(8,128)S(1)}, u32[]{:S(2)}) copy-start(f32[1024,1024]{1,0:T(8,128)S(1)} %convolution_multiply_fusion) | copy-start | bytes 12582916
  90.8 3.1 %copy-start.18 = (bf16[8,1,128,1024]{3,2,1,0:T(8,128)(2,1)S(1)}, bf16[8,1,128,1024]{3,2,1,0:T(8,128)(2,1)}, u32[]{:S(2)}) copy-start(bf16[8,1,128,1024]{3,2,1,0:T(8,128)(2,1)} %copy-done.17) | copy-start | bytes 6291460
  91.9 7.8 %collective-permute-start.11 = (bf16[8,2,32,1024]{3,2,1,0:T(8,128)(2,1)}, bf16[8,2,32,1024]{3,2,1,0:T(8,128)(2,1)}, u32[]{:S(2)}, u32[]{:S(2)}) collective-permute-start(bf16[8,2,32,1024]{3,2,1,0:T(8,128)(2,1)} %fusion.4), channel_id=1, source_target_pairs={{0,8},{8,0},{1,9},{9,1},{2,10},{10,2},{3,11},{11,3},{4,12},{12,4},... | collective-permute-start | bytes 3145736 | tf_op jit(solution)/shard_map/ppermute | solution.py:166
  96.3 2.0 %copy-start.14 = (f32[1024,1024]{1,0:T(8,128)}, f32[1024,1024]{1,0:T(8,128)S(1)}, u32[]{:S(2)}) copy-start(f32[1024,1024]{1,0:T(8,128)S(1)} %fusion.18) | copy-start | bytes 12582916
  99.4 3.0 %collective-permute-start.10 = (bf16[8,2,32,1024]{3,2,1,0:T(8,128)(2,1)}, bf16[8,2,32,1024]{3,2,1,0:T(8,128)(2,1)}, u32[]{:S(2)}, u32[]{:S(2)}) collective-permute-start(bf16[8,2,32,1024]{3,2,1,0:T(8,128)(2,1)} %fusion.3), channel_id=1, source_target_pairs={{0,8},{8,0},{1,9},{9,1},{2,10},{10,2},{3,11},{11,3},{4,12},{12,4},... | collective-permute-start | bytes 3145736 | tf_op jit(solution)/shard_map/ppermute | solution.py:166
  99.7 3.1 %copy-start.15 = (f32[1024,1024]{1,0:T(8,128)S(1)}, f32[1024,1024]{1,0:T(8,128)}, u32[]{:S(2)}) copy-start(f32[1024,1024]{1,0:T(8,128)} %copy-done.14) | copy-start | bytes 12582916
  102.1 2.3 %copy-start.9 = (bf16[8,2,32,1024]{3,2,1,0:T(8,128)(2,1)}, bf16[8,2,32,1024]{3,2,1,0:T(8,128)(2,1)S(1)}, u32[]{:S(2)}) copy-start(bf16[8,2,32,1024]{3,2,1,0:T(8,128)(2,1)S(1)} %fusion.1) | copy-start | bytes 3145732
  105.8 30.0 %copy-start.5 = (f32[1,1024]{1,0:T(1,128)S(1)}, f32[1,1024]{1,0:T(1,128)}, u32[]{:S(2)}) copy-start(f32[1,1024]{1,0:T(1,128)} %eig_cols.1) | copy-start | bytes 12292
  105.8 32.0 %collective-permute-start.12 = (bf16[8,64,1024]{2,1,0:T(8,128)(2,1)}, bf16[8,64,1024]{2,1,0:T(8,128)(2,1)}, u32[]{:S(2)}, u32[]{:S(2)}) collective-permute-start(bf16[8,64,1024]{2,1,0:T(8,128)(2,1)} %fusion.6), channel_id=1, source_target_pairs={{0,16},{16,0},{1,17},{17,1},{2,18},{18,2},{3,19},{19,3},{4,20},{20... | collective-permute-start | bytes 3145736 | tf_op jit(solution)/shard_map/ppermute | solution.py:166
  112.3 23.5 %all-to-all-start.2 = ((bf16[8,32,1024]{2,1,0:T(8,128)(2,1)}), bf16[8,32,1024]{2,1,0:T(8,128)(2,1)S(1)}, u32[]{:S(2)}, u32[]{:S(2)}) async-start(bf16[8,32,1024]{2,1,0:T(8,128)(2,1)} %copy-done.2), calls=%async_computation.2 | async-start | bytes 1048576 | tf_op jit(solution)/shard_map/all_to_all | solution.py:212
  135.8 2.1 %copy-start.10 = (bf16[8,2,32,1024]{3,2,1,0:T(8,128)(2,1)S(1)}, bf16[8,2,32,1024]{3,2,1,0:T(8,128)(2,1)}, u32[]{:S(2)}) copy-start(bf16[8,2,32,1024]{3,2,1,0:T(8,128)(2,1)} %copy-done.9) | copy-start | bytes 3145732
  135.8 2.1 %copy-start.12 = (bf16[8,2,32,1024]{3,2,1,0:T(8,128)(2,1)S(1)}, bf16[8,2,32,1024]{3,2,1,0:T(8,128)(2,1)}, u32[]{:S(2)}) copy-start(bf16[8,2,32,1024]{3,2,1,0:T(8,128)(2,1)} %copy-done.11) | copy-start | bytes 3145732
  137.3 3.3 %collective-permute-start.13 = (f32[64,1024]{1,0:T(8,128)S(1)}, f32[64,1024]{1,0:T(8,128)S(1)}, u32[]{:S(2)}, u32[]{:S(2)}) collective-permute-start(f32[64,1024]{1,0:T(8,128)S(1)} %dynamic-slice_bitcast_fusion), channel_id=1, source_target_pairs={{0,8},{8,0},{1,9},{9,1},{2,10},{10,2},{3,11},{11,3},{4,12},{12,4},... | collective-permute-start | bytes 786440 | tf_op jit(solution)/shard_map/ppermute | solution.py:166
  140.6 13.8 %copy-start.27 = (s32[8]{0:T(128)S(1)}, s32[8]{0:T(128)}, u32[]{:S(2)}) copy-start(s32[8]{0:T(128)} %assign.1) | copy-start | bytes 100
  140.6 32.8 %all-to-all-start.3 = ((bf16[8,64,1024]{2,1,0:T(8,128)(2,1)}), bf16[8,64,1024]{2,1,0:T(8,128)(2,1)S(1)}, u32[]{:S(2)}, u32[]{:S(2)}) async-start(bf16[8,64,1024]{2,1,0:T(8,128)(2,1)} %fusion), calls=%async_computation.3 | async-start | bytes 2097152 | tf_op jit(solution)/shard_map/all_to_all | solution.py:230
  144.2 5.2 %collective-permute-start.14 = (f32[32,1024]{1,0:T(8,128)S(1)}, f32[32,1024]{1,0:T(8,128)S(1)}, u32[]{:S(2)}, u32[]{:S(2)}) collective-permute-start(f32[32,1024]{1,0:T(8,128)S(1)} %dynamic-slice_bitcast_fusion.1), channel_id=1, source_target_pairs={{0,16},{16,0},{1,17},{17,1},{2,18},{18,2},{3,19},{19,3},{4,20},{20... | collective-permute-start | bytes 393224 | tf_op jit(solution)/shard_map/ppermute | solution.py:166
  149.4 8.8 %collective-permute-start.15 = (bf16[32,1024]{1,0:T(8,128)(2,1)S(1)}, bf16[32,1024]{1,0:T(8,128)(2,1)S(1)}, u32[]{:S(2)}, u32[]{:S(2)}) collective-permute-start(bf16[32,1024]{1,0:T(8,128)(2,1)S(1)} %fusion.11), channel_id=1, source_target_pairs={{0,7},{1,0},{2,1},{3,2},{4,3},{5,4},{6,5},{7,6},{8,15},{9,8},{10,9... | collective-permute-start | bytes 196616 | tf_op jit(solution)/shard_map/ppermute | solution.py:235
  153.3 8.7 %collective-permute-start.16 = (bf16[32,1024]{1,0:T(8,128)(2,1)S(1)}, bf16[32,1024]{1,0:T(8,128)(2,1)S(1)}, u32[]{:S(2)}, u32[]{:S(2)}) collective-permute-start(bf16[32,1024]{1,0:T(8,128)(2,1)S(1)} %fusion.11), channel_id=1, source_target_pairs={{0,6},{1,7},{2,0},{3,1},{4,2},{5,3},{6,4},{7,5},{8,14},{9,15},{10,... | collective-permute-start | bytes 196616 | tf_op jit(solution)/shard_map/ppermute | solution.py:235
  154.4 7.7 %collective-permute-start.17 = (bf16[32,1024]{1,0:T(8,128)(2,1)S(1)}, bf16[32,1024]{1,0:T(8,128)(2,1)S(1)}, u32[]{:S(2)}, u32[]{:S(2)}) collective-permute-start(bf16[32,1024]{1,0:T(8,128)(2,1)S(1)} %fusion.11), channel_id=1, source_target_pairs={{0,5},{1,6},{2,7},{3,0},{4,1},{5,2},{6,3},{7,4},{8,13},{9,14},{10,... | collective-permute-start | bytes 196616 | tf_op jit(solution)/shard_map/ppermute | solution.py:235
  155.8 6.3 %collective-permute-start.18 = (bf16[32,1024]{1,0:T(8,128)(2,1)S(1)}, bf16[32,1024]{1,0:T(8,128)(2,1)S(1)}, u32[]{:S(2)}, u32[]{:S(2)}) collective-permute-start(bf16[32,1024]{1,0:T(8,128)(2,1)S(1)} %fusion.11), channel_id=1, source_target_pairs={{0,4},{1,5},{2,6},{3,7},{4,0},{5,1},{6,2},{7,3},{8,12},{9,13},{10,... | collective-permute-start | bytes 196616 | tf_op jit(solution)/shard_map/ppermute | solution.py:235
  157.3 6.1 %collective-permute-start.19 = (bf16[32,1024]{1,0:T(8,128)(2,1)S(1)}, bf16[32,1024]{1,0:T(8,128)(2,1)S(1)}, u32[]{:S(2)}, u32[]{:S(2)}) collective-permute-start(bf16[32,1024]{1,0:T(8,128)(2,1)S(1)} %fusion.11), channel_id=1, source_target_pairs={{0,3},{1,4},{2,5},{3,6},{4,7},{5,0},{6,1},{7,2},{8,11},{9,12},{10,... | collective-permute-start | bytes 196616 | tf_op jit(solution)/shard_map/ppermute | solution.py:235
  158.2 7.1 %collective-permute-start.20 = (bf16[32,1024]{1,0:T(8,128)(2,1)S(1)}, bf16[32,1024]{1,0:T(8,128)(2,1)S(1)}, u32[]{:S(2)}, u32[]{:S(2)}) collective-permute-start(bf16[32,1024]{1,0:T(8,128)(2,1)S(1)} %fusion.11), channel_id=1, source_target_pairs={{0,2},{1,3},{2,4},{3,5},{4,6},{5,7},{6,0},{7,1},{8,10},{9,11},{10,... | collective-permute-start | bytes 196616 | tf_op jit(solution)/shard_map/ppermute | solution.py:235
  162.1 7.3 %collective-permute-start.21 = (bf16[32,1024]{1,0:T(8,128)(2,1)S(1)}, bf16[32,1024]{1,0:T(8,128)(2,1)S(1)}, u32[]{:S(2)}, u32[]{:S(2)}) collective-permute-start(bf16[32,1024]{1,0:T(8,128)(2,1)S(1)} %fusion.11), channel_id=1, source_target_pairs={{0,1},{1,2},{2,3},{3,4},{4,5},{5,6},{6,7},{7,0},{8,9},{9,10},{10,1... | collective-permute-start | bytes 196616 | tf_op jit(solution)/shard_map/ppermute | solution.py:235
  (6 other events, 6.9 us)
where the time goes:
time: 175 us; the launch traced here: 174 us
  waiting for transfers between devices  59.6 us (34%)
  starting transfers between devices  56.7 us (32%)
  local copies, waits for them, and re-layouts  20.3 us (12%)
  matrix products  13.8 us (8%)
  other arithmetic  12.5 us (7%)
  Pallas kernels  10.4 us (6%)
    ppermute x4, waiting for transfers between devices, body(): lax.ppermute(up, 'z', [(i, (i + 1) % n_z) for i in range(n_z)])  20.5 us
    all_to_all x1, waiting for transfers between devices, body(): lax.all_to_all(spread, 'z', 0, 0, tiled=True).reshape(n_z * rows, width)  16.9 us
    ppermute x7, starting transfers between devices, body(): lax.ppermute(result, GRP, [(i, (i + s) % n_grp) for i in range(n_grp)])  12.6 us
    unnamed x57, local copies, waits for them, and re-layouts  12.5 us
    dot_general x4, matrix products, dot_first(): return lax.dot_general(x, y, contract_first, preferred_element_type=f32)  11.5 us
    ppermute x8, starting transfers between devices, swap(): return lax.ppermute(x, axis, [(0, 1), (1, 0)])  11 us
    ppermute x3, starting transfers between devices, body(): lax.ppermute(down, 'z', [(i, (i - 1) % n_z) for i in range(n_z)])  9.36 us
    ppermute x8, waiting for transfers between devices, swap(): return lax.ppermute(x, axis, [(0, 1), (1, 0)])  8.19 us
  transfers between devices with their start and end apart: 26, of which 13 were waited for; matrix products, arithmetic and copies ran while one was open for 13% of the time, Pallas kernels for 6%

commit v1 on v0

--- a/solution.py
+++ b/solution.py
@@ -168,9 +168,11 @@
     def in_order(index, mine, other):
         return jnp.where(index == 0, mine, other), jnp.where(index == 0, other, mine)
 
-    mine = jnp.stack([bases_g[0], bases_a[0]])
-    other, send = lax.optimization_barrier((swap(mine, "xl"), pick(assign, grads, acts)))
-    mine = jnp.stack(in_order(xl, mine, other), axis=1)
+    mine = bases_g[0], bases_a[0]
+    other, send = lax.optimization_barrier(
+        ([swap(x, "xl") for x in mine], pick(assign, grads, acts))
+    )
+    mine = jnp.stack([jnp.stack(in_order(xl, *x)) for x in zip(mine, other)])
     pieces = [mine] * n_z
     up = down = mine
     for s in range(1, n_z // 2 + 1):
@@ -207,7 +209,10 @@
     own_g, own_a, pair = lax.optimization_barrier((own_g, own_a, pair))
     half_g = core_sum(dot_first(own_g, own_g))
     half_a = core_sum(dot_first(own_a, own_a) / tokens)
-    halves = half_sum(jnp.concatenate([half_g, half_a], axis=2), "xl", xl, 1)
+    halves = jnp.concatenate([half_g, half_a], axis=2)
+    keep = lax.optimization_barrier(lax.dynamic_index_in_dim(halves, xl, 1, False))
+    give = swap(lax.dynamic_index_in_dim(halves, 1 - xl, 1, False), "xl")
+    halves = (keep.astype(f32) + give.astype(f32)).astype(bf16)
     spread = spread_sum(lax.all_to_all(pair, ("xl", "z"), 0, 0, tiled=True), n_z)
     rotated = lax.all_to_all(spread, "z", 0, 0, tiled=True).reshape(n_z * rows, width)
 
@@ -230,11 +235,20 @@
     sums = jnp.sum(lax.all_to_all(halves, "z", 0, 0, tiled=True).astype(f32), axis=0)
     factor_g, factor_a = sums[:rows], sums[rows:]
     result = fold(result, "xl", xl).astype(bf16)
-    pieces = [result]
-    for s in range(1, n_grp):
-        pieces.append(lax.ppermute(result, GRP, [(i, (i + s) % n_grp) for i in range(n_grp)]))
-    me = lax.axis_index(GRP)
-    index = lax.rem(me - assign + n_grp, n_grp)[:, None, None]
+    n_y = lax.axis_size("y")
+    pieces = [result] * n_grp
+    hops = sorted(
+        range(1, n_grp), key=lambda s: -(2 * (s // n_y) + min(s % n_y, n_y - s % n_y))
+    )
+    for s in hops:
+        dx, dy = s // n_y, s % n_y
+        moves = [
+            (i, (i // n_y + dx) % (n_grp // n_y) * n_y + (i + dy) % n_y) for i in range(n_grp)
+        ]
+        pieces[s] = lax.ppermute(result, GRP, moves)
+    dx = lax.rem(lax.axis_index("xh") - assign // n_y + n_grp // n_y, n_grp // n_y)
+    dy = lax.rem(lax.axis_index("y") - lax.rem(assign, n_y) + n_y, n_y)
+    index = (dx * n_y + dy)[:, None, None]
     precond = jnp.broadcast_to(pieces[0][None], (n_proj, rows, width))
     for s in range(1, n_grp):
         precond = jnp.where(index == s, pieces[s][None], precond)

time: 175 us -> 174 us (level)
    ppermute x7, waiting for transfers between devices: 7.31 us -> 4.32 us  [body(): pieces[s] = lax.ppermute(result, GRP, moves)]
    all_to_all x1, waiting for transfers between devices: 2.81 us -> 5.8 us  [body(): lax.all_to_all(halves, 'z', 0, 0, tiled=True).astype(f32)]
    convert_element_type x3 -> x2, other arithmetic: 6.72 us -> 4.01 us  [half_sum(): (keep.astype(f32) + swap(give.astype(bf16), axis).astype(f32)).astype(bf16)]
    convert_element_type x0 -> x1, other arithmetic: none -> 2.66 us  [body(): halves = (keep.astype(f32) + give.astype(f32)).astype(bf16)]
    unnamed x57 -> x54, local copies, waits for them, and re-layouts: 12.5 us -> 11.7 us
    ppermute x8 -> x9, starting transfers between devices: 11 us -> 11.4 us  [swap(): return lax.ppermute(x, axis, [(0, 1), (1, 0)])]
    ppermute x8 -> x9, waiting for transfers between devices: 8.19 us -> 8.2 us  [swap(): return lax.ppermute(x, axis, [(0, 1), (1, 0)])]
  transfers between devices with their start and end apart: 26 -> 27, of which waited for: 13 -> 13; matrix products, arithmetic and copies ran while one was open for 13% -> 14% of each run, Pallas kernels for 6% -> 6%
where the time goes in v1:
time: 174 us; the launch traced here: 173 us
  waiting for transfers between devices  58.9 us (34%)
  starting transfers between devices  58 us (33%)
  local copies, waits for them, and re-layouts  18.6 us (11%)
  matrix products  13.8 us (8%)
  other arithmetic  12.7 us (7%)
  Pallas kernels  10.4 us (6%)
    ppermute x4, waiting for transfers between devices, body(): lax.ppermute(up, 'z', [(i, (i + 1) % n_z) for i in range(n_z)])  19.9 us
    all_to_all x1, waiting for transfers between devices, body(): lax.all_to_all(spread, 'z', 0, 0, tiled=True).reshape(n_z * rows, width)  16.9 us
    ppermute x7, starting transfers between devices, body(): pieces[s] = lax.ppermute(result, GRP, moves)  12.6 us
    unnamed x54, local copies, waits for them, and re-layouts  11.7 us
    dot_general x4, matrix products, dot_first(): return lax.dot_general(x, y, contract_first, preferred_element_type=f32)  11.5 us
    ppermute x9, starting transfers between devices, swap(): return lax.ppermute(x, axis, [(0, 1), (1, 0)])  11.4 us
    ppermute x3, starting transfers between devices, body(): lax.ppermute(down, 'z', [(i, (i - 1) % n_z) for i in range(n_z)])  9.35 us
    ppermute x9, waiting for transfers between devices, swap(): return lax.ppermute(x, axis, [(0, 1), (1, 0)])  8.2 us
  transfers between devices with their start and end apart: 27, of which 13 were waited for; matrix products, arithmetic and copies ran while one was open for 14% of the time, Pallas kernels for 6%

profile of v1, /device:TPU:1, one launch (start us, length us, event | category | flops | bytes accessed | tf_op | source)
XLA Modules:
  0.0 173.4 jit_solution(4223879117373580082)
XLA Ops:
  0.6 2.1 %collective-permute-start = (bf16[32,1024]{1,0:T(8,128)(2,1)}, bf16[32,1024]{1,0:T(8,128)(2,1)S(1)}, u32[]{:S(2)}, u32[]{:S(2)}) collective-permute-start(bf16[32,1024]{1,0:T(8,128)(2,1)} %bitcast.98), channel_id=1, source_target_pairs={{0,16},{16,0},{1,17},{17,1},{2,18},{18,2},{3,19},{19,3},{4,20},{20... | collective-permute-start | bytes 196616 | tf_op jit(solution)/shard_map/ppermute | solution.py:166
  2.9 4.6 %shard_map.94 = bf16[8,2,128,1024]{3,2,1,0:T(8,128)(2,1)} custom-call(s32[8]{0:T(128)} %assign.1, bf16[8,128,1024]{2,1,0:T(8,128)(2,1)} %grads.1, bf16[8,128,1024]{2,1,0:T(8,128)(2,1)} %acts.1), custom_call_target="tpu_custom_call" | custom-call | bytes 8388608 | tf_op jit(solution)/shard_map/pallas_call | solution.py:38
  7.5 6.9 %all-to-all-start = ((bf16[8,2,128,1024]{3,2,1,0:T(8,128)(2,1)}), bf16[8,2,128,1024]{3,2,1,0:T(8,128)(2,1)}, u32[]{:S(2)}, u32[]{:S(2)}) async-start(bf16[8,2,128,1024]{3,2,1,0:T(8,128)(2,1)} %shard_map.94), calls=%async_computation | async-start | bytes 8388608 | tf_op jit(solution)/shard_map/all_to_all | solution.py:185
  14.6 1.7 collective-permute-start.2
  16.3 4.0 %collective-permute-start.6 = (bf16[2,2,32,1024]{3,2,1,0:T(8,128)(2,1)S(1)}, bf16[2,2,32,1024]{3,2,1,0:T(8,128)(2,1)S(1)}, u32[]{:S(2)}, u32[]{:S(2)}) collective-permute-start(bf16[2,2,32,1024]{3,2,1,0:T(8,128)(2,1)S(1)} %pad_maximum_fusion.refs_0_), channel_id=1, source_target_pairs={{0,224},{32,0},{64,32},{96,64},{128,96},{160,128},{192,160},{224,1... | collective-permute-start | bytes 786440 | tf_op jit(solution)/shard_map/ppermute | solution.py:181
  20.3 5.1 %collective-permute-done.2.refs_1_ = bf16[2,2,32,1024]{3,2,1,0:T(8,128)(2,1)S(1)} collective-permute-done((bf16[2,2,32,1024]{3,2,1,0:T(8,128)(2,1)S(1)}, bf16[2,2,32,1024]{3,2,1,0:T(8,128)(2,1)S(1)}, u32[]{:S(2)}, u32[]{:S(2)}) %collective-permute-start.2) | collective-permute-done | bytes 262176 | tf_op jit(solution)/shard_map/ppermute | solution.py:179
  25.5 2.7 %collective-permute-start.7 = (bf16[2,2,32,1024]{3,2,1,0:T(8,128)(2,1)S(1)}, bf16[2,2,32,1024]{3,2,1,0:T(8,128)(2,1)S(1)}, u32[]{:S(2)}, u32[]{:S(2)}) collective-permute-start(bf16[2,2,32,1024]{3,2,1,0:T(8,128)(2,1)S(1)} %collective-permute-done.6.refs_7_), channel_id=1, source_target_pairs={{0,224},{32,0},{64,32},{96,64},{128,96},{160,128},{192,160},{224,1... | collective-permute-start | bytes 786440 | tf_op jit(solution)/shard_map/ppermute | solution.py:181
  28.1 4.4 %collective-permute-done.3.refs_2_ = bf16[2,2,32,1024]{3,2,1,0:T(8,128)(2,1)S(1)} collective-permute-done((bf16[2,2,32,1024]{3,2,1,0:T(8,128)(2,1)S(1)}, bf16[2,2,32,1024]{3,2,1,0:T(8,128)(2,1)S(1)}, u32[]{:S(2)}, u32[]{:S(2)}) %collective-permute-start.3) | collective-permute-done | bytes 262176 | tf_op jit(solution)/shard_map/ppermute | solution.py:179
  32.5 2.7 %collective-permute-start.8 = (bf16[2,2,32,1024]{3,2,1,0:T(8,128)(2,1)S(1)}, bf16[2,2,32,1024]{3,2,1,0:T(8,128)(2,1)S(1)}, u32[]{:S(2)}, u32[]{:S(2)}) collective-permute-start(bf16[2,2,32,1024]{3,2,1,0:T(8,128)(2,1)S(1)} %collective-permute-done.7.refs_6_), channel_id=1, source_target_pairs={{0,224},{32,0},{64,32},{96,64},{128,96},{160,128},{192,160},{224,1... | collective-permute-start | bytes 786440 | tf_op jit(solution)/shard_map/ppermute | solution.py:181
  35.2 4.2 %collective-permute-done.4.refs_3_ = bf16[2,2,32,1024]{3,2,1,0:T(8,128)(2,1)S(1)} collective-permute-done((bf16[2,2,32,1024]{3,2,1,0:T(8,128)(2,1)S(1)}, bf16[2,2,32,1024]{3,2,1,0:T(8,128)(2,1)S(1)}, u32[]{:S(2)}, u32[]{:S(2)}) %collective-permute-start.4) | collective-permute-done | bytes 262176 | tf_op jit(solution)/shard_map/ppermute | solution.py:179
  39.9 6.3 %collective-permute-done.5.refs_4_ = bf16[2,2,32,1024]{3,2,1,0:T(8,128)(2,1)S(1)} collective-permute-done((bf16[2,2,32,1024]{3,2,1,0:T(8,128)(2,1)S(1)}, bf16[2,2,32,1024]{3,2,1,0:T(8,128)(2,1)S(1)}, u32[]{:S(2)}, u32[]{:S(2)}) %collective-permute-start.5) | collective-permute-done | bytes 262176 | tf_op jit(solution)/shard_map/ppermute | solution.py:179
  47.0 3.6 %shard_map.95.mine = bf16[8,2,2,32,1024]{4,3,2,1,0:T(8,128)(2,1)} custom-call(s32[8]{0:T(128)} %compare_select_fusion.4.index, bf16[2,2,32,1024]{3,2,1,0:T(8,128)(2,1)} %copy-done.16, bf16[2,2,32,1024]{3,2,1,0:T(8,128)(2,1)} %copy-done.17, bf16[2,2,32,1024]{3,2,1,0:T(8,128)(2,1)} %copy-done.19, bf16[2,2,32,1024]{3,2,1,0:T(8,128)(2,1)} %copy-done.21, ...), custom_call_target="tpu_custom_call" | custom-call | tf_op jit(solution)/shard_map/pallas_call | solution.py:70
  50.6 4.5 %collective-permute-start.9 = (bf16[8,2,2,32,1024]{4,3,2,1,0:T(8,128)(2,1)}, bf16[8,2,2,32,1024]{4,3,2,1,0:T(8,128)(2,1)S(1)}, u32[]{:S(2)}, u32[]{:S(2)}) collective-permute-start(bf16[8,2,2,32,1024]{4,3,2,1,0:T(8,128)(2,1)} %shard_map.95.mine), channel_id=1, source_target_pairs={{0,8},{8,0},{1,9},{9,1},{2,10},{10,2},{3,11},{11,3},{4,12},{12,4},... | collective-permute-start | bytes 6291464 | tf_op jit(solution)/shard_map/ppermute | solution.py:166
  55.0 4.0 %collective-permute-done.9.other = bf16[8,2,2,32,1024]{4,3,2,1,0:T(8,128)(2,1)S(1)} collective-permute-done((bf16[8,2,2,32,1024]{4,3,2,1,0:T(8,128)(2,1)}, bf16[8,2,2,32,1024]{4,3,2,1,0:T(8,128)(2,1)S(1)}, u32[]{:S(2)}, u32[]{:S(2)}) %collective-permute-start.9) | collective-permute-done | bytes 2097184 | tf_op jit(solution)/shard_map/ppermute | solution.py:166
  59.0 1.4 copy-done.3
  60.5 1.6 copy-done.1
  62.1 1.6 copy-done.4
  64.3 1.3 copy-done.6
  65.6 2.8 %fusion.20 = (bf16[8,1,128,1024]{3,2,1,0:T(8,128)(2,1)S(1)}, bf16[8,1,128,1024]{3,2,1,0:T(8,128)(2,1)S(1)}) fusion(bf16[8,2,128,1024]{3,2,1,0:T(8,128)(2,1)} %all-to-all-done), kind=kLoop, calls=%fused_computation.66 | loop fusion | bytes 8388608 | tf_op jit(solution)/shard_map/slice | solution.py:188
  68.5 2.3 %convolution_convert_fusion = bf16[1024,1024]{1,0:T(8,128)(2,1)S(1)} fusion(bf16[1024,1024]{1,0:T(8,128)(2,1)S(1)} %bitcast.92, bf16[1024,1024]{1,0:T(8,128)(2,1)S(1)} %bitcast.83), kind=kOutput, calls=%fused_computation.14 | convolution fusion | flops 2148532224 | bytes 6291456 | tf_op jit(solution)/shard_map/dot_general | solution.py:201
  70.9 1.3 convolution_convert_fusion.1
  72.8 3.2 %convolution_convert_fusion.2 = bf16[512,1024]{1,0:T(8,128)(2,1)S(1)} fusion(bf16[1024,1024]{1,0:T(8,128)(2,1)} %bitcast.85, bf16[1024,1024]{1,0:T(8,128)(2,1)} %copy-done.13, s32[]{:T(128)S(6)} %select_n.87), kind=kOutput, calls=%fused_computation.16 | convolution fusion | flops 1074266112 | bytes 4194308 | tf_op jit(solution)/shard_map/dot_general | solution.py:191
  76.0 2.5 %add_convert_fusion.1 = bf16[512,1024]{1,0:T(8,128)(2,1)} fusion(bf16[512,1024]{1,0:T(8,128)(2,1)} %collective-permute-done.10, bf16[512,1024]{1,0:T(8,128)(2,1)S(1)} %convolution_convert_fusion.2), kind=kLoop, calls=%fused_computation.13 | loop fusion | flops 2097152 | bytes 3145728 | tf_op jit(solution)/shard_map/convert_element_type | solution.py:207
  78.5 6.7 %all-to-all-start.1 = ((bf16[16,32,1024]{2,1,0:T(8,128)(2,1)}), bf16[16,32,1024]{2,1,0:T(8,128)(2,1)S(1)}, u32[]{:S(2)}, u32[]{:S(2)}) async-start(bf16[16,32,1024]{2,1,0:T(8,128)(2,1)} %bitcast.87), calls=%async_computation.1 | async-start | bytes 2097152 | tf_op jit(solution)/shard_map/all_to_all | solution.py:216
  85.3 4.6 %convolution_multiply_fusion = f32[1024,1024]{1,0:T(8,128)S(1)} fusion(bf16[1024,1024]{1,0:T(8,128)(2,1)} %bitcast.86), kind=kOutput, calls=%fused_computation.4 | convolution fusion | flops 2148532224 | bytes 6291456 | tf_op jit(solution)/shard_map/dot_general | solution.py:191
  91.4 1.7 copy-done.15
  93.0 2.4 %fusion.21 = f32[1024,1024]{1,0:T(8,128)S(1)} fusion(bf16[1024,1024]{1,0:T(8,128)(2,1)S(1)} %bitcast.93), kind=kOutput, calls=%fused_computation.67 | convolution fusion | flops 2147483648 | bytes 6291456 | tf_op jit(solution)/shard_map/dot_general | solution.py:191
  95.4 2.0 %copy-done.11 = f32[1024,1024]{1,0:T(8,128)} copy-done((f32[1024,1024]{1,0:T(8,128)}, f32[1024,1024]{1,0:T(8,128)S(1)}, u32[]{:S(2)}) %copy-start.11) | copy-done | bytes 4194328
  98.9 2.4 %fusion = bf16[8,2,32,1024]{3,2,1,0:T(8,128)(2,1)S(1)} fusion(bf16[8,2,32,1024]{3,2,1,0:T(8,128)(2,1)} %collective-permute-done.12, f32[8,2,2,32,1024]{4,3,2,1,0:T(8,128)} %bitcast.89, s32[]{:T(128)S(6)} %select_n.89), kind=kLoop, calls=%fused_computation.7 | loop fusion | flops 1572864 | bytes 4194308 | tf_op jit(solution)/shard_map/convert_element_type | solution.py:196
  102.0 1.6 fusion.1
  103.7 1.5 fusion.7
  105.1 1.6 collective-permute-start.13
  106.8 3.7 %all-to-all-done.1.src = bf16[16,32,1024]{2,1,0:T(8,128)(2,1)S(1)} async-done(((bf16[16,32,1024]{2,1,0:T(8,128)(2,1)}), bf16[16,32,1024]{2,1,0:T(8,128)(2,1)S(1)}, u32[]{:S(2)}, u32[]{:S(2)}) %all-to-all-start.1) | async-done | bytes 1048608 | tf_op jit(solution)/shard_map/all_to_all | solution.py:216
  111.4 5.5 %all-to-all-start.2 = ((bf16[8,32,1024]{2,1,0:T(8,128)(2,1)}), bf16[8,32,1024]{2,1,0:T(8,128)(2,1)S(1)}, u32[]{:S(2)}, u32[]{:S(2)}) async-start(bf16[8,32,1024]{2,1,0:T(8,128)(2,1)} %copy-done.2), calls=%async_computation.2 | async-start | bytes 1048576 | tf_op jit(solution)/shard_map/all_to_all | solution.py:217
  118.0 16.9 %all-to-all-done.2 = bf16[8,32,1024]{2,1,0:T(8,128)(2,1)S(1)} async-done(((bf16[8,32,1024]{2,1,0:T(8,128)(2,1)}), bf16[8,32,1024]{2,1,0:T(8,128)(2,1)S(1)}, u32[]{:S(2)}, u32[]{:S(2)}) %all-to-all-start.2) | async-done | bytes 524320 | tf_op jit(solution)/shard_map/all_to_all | solution.py:217
  134.9 1.4 shard_map.98
  137.0 2.7 %add_convert_fusion = bf16[8,64,1024]{2,1,0:T(8,128)(2,1)} fusion(bf16[8,64,1024]{2,1,0:T(8,128)(2,1)} %collective-permute-done.13, bf16[8,64,1024]{2,1,0:T(8,128)(2,1)S(1)} %copy-done.9), kind=kLoop, calls=%fused_computation.11 | loop fusion | flops 2097152 | bytes 3145728 | tf_op jit(solution)/shard_map/convert_element_type | solution.py:215
  139.7 3.6 %all-to-all-start.3 = ((bf16[8,64,1024]{2,1,0:T(8,128)(2,1)}), bf16[8,64,1024]{2,1,0:T(8,128)(2,1)S(1)}, u32[]{:S(2)}, u32[]{:S(2)}) async-start(bf16[8,64,1024]{2,1,0:T(8,128)(2,1)} %add_convert_fusion), calls=%async_computation.3 | async-start | bytes 2097152 | tf_op jit(solution)/shard_map/all_to_all | solution.py:235
  143.3 1.3 collective-permute-start.15
  144.6 3.9 %collective-permute-done.15 = f32[32,1024]{1,0:T(8,128)S(1)} collective-permute-done((f32[32,1024]{1,0:T(8,128)S(1)}, f32[32,1024]{1,0:T(8,128)S(1)}, u32[]{:S(2)}, u32[]{:S(2)}) %collective-permute-start.15) | collective-permute-done | bytes 131104 | tf_op jit(solution)/shard_map/ppermute | solution.py:166
  148.5 4.4 %collective-permute-start.16 = (bf16[32,1024]{1,0:T(8,128)(2,1)S(1)}, bf16[32,1024]{1,0:T(8,128)(2,1)S(1)}, u32[]{:S(2)}, u32[]{:S(2)}) collective-permute-start(bf16[32,1024]{1,0:T(8,128)(2,1)S(1)} %fusion.10), channel_id=1, source_target_pairs={{0,7},{1,4},{2,5},{3,6},{4,3},{5,0},{6,1},{7,2},{8,15},{9,12},{10,... | collective-permute-start | bytes 196616 | tf_op jit(solution)/shard_map/ppermute | solution.py:248
  152.9 1.3 collective-permute-start.17
  154.3 2.3 %collective-permute-start.18 = (bf16[32,1024]{1,0:T(8,128)(2,1)S(1)}, bf16[32,1024]{1,0:T(8,128)(2,1)S(1)}, u32[]{:S(2)}, u32[]{:S(2)}) collective-permute-start(bf16[32,1024]{1,0:T(8,128)(2,1)S(1)} %fusion.10), channel_id=1, source_target_pairs={{0,5},{1,6},{2,7},{3,4},{4,1},{5,2},{6,3},{7,0},{8,13},{9,14},{10,... | collective-permute-start | bytes 196616 | tf_op jit(solution)/shard_map/ppermute | solution.py:248
  157.5 2.1 %collective-permute-start.20 = (bf16[32,1024]{1,0:T(8,128)(2,1)S(1)}, bf16[32,1024]{1,0:T(8,128)(2,1)S(1)}, u32[]{:S(2)}, u32[]{:S(2)}) collective-permute-start(bf16[32,1024]{1,0:T(8,128)(2,1)S(1)} %fusion.10), channel_id=1, source_target_pairs={{0,3},{1,0},{2,1},{3,2},{4,7},{5,4},{6,5},{7,6},{8,11},{9,8},{10,9... | collective-permute-start | bytes 196616 | tf_op jit(solution)/shard_map/ppermute | solution.py:248
  159.7 1.5 collective-permute-start.21
  162.0 2.3 %collective-permute-done.21 = bf16[32,1024]{1,0:T(8,128)(2,1)S(1)} collective-permute-done((bf16[32,1024]{1,0:T(8,128)(2,1)S(1)}, bf16[32,1024]{1,0:T(8,128)(2,1)S(1)}, u32[]{:S(2)}, u32[]{:S(2)}) %collective-permute-start.21) | collective-permute-done | bytes 65568 | tf_op jit(solution)/shard_map/ppermute | solution.py:248
  164.3 1.2 collective-permute-done.22
  166.7 5.8 %all-to-all-done.3 = bf16[8,64,1024]{2,1,0:T(8,128)(2,1)S(1)} async-done(((bf16[8,64,1024]{2,1,0:T(8,128)(2,1)}), bf16[8,64,1024]{2,1,0:T(8,128)(2,1)S(1)}, u32[]{:S(2)}, u32[]{:S(2)}) %all-to-all-start.3) | async-done | bytes 1048608 | tf_op jit(solution)/shard_map/all_to_all | solution.py:235
  (96 shorter events, 13.0 us)
Async XLA Ops:
  0.6 116.3 %copy-start = (f32[1,1024]{1,0:T(1,128)S(1)}, f32[1,1024]{1,0:T(1,128)}, u32[]{:S(2)}) copy-start(f32[1,1024]{1,0:T(1,128)} %param.13) | copy-start | bytes 12292
  0.6 6.8 %collective-permute-start = (bf16[32,1024]{1,0:T(8,128)(2,1)}, bf16[32,1024]{1,0:T(8,128)(2,1)S(1)}, u32[]{:S(2)}, u32[]{:S(2)}) collective-permute-start(bf16[32,1024]{1,0:T(8,128)(2,1)} %bitcast.98), channel_id=1, source_target_pairs={{0,16},{16,0},{1,17},{17,1},{2,18},{18,2},{3,19},{19,3},{4,20},{20... | collective-permute-start | bytes 196616 | tf_op jit(solution)/shard_map/ppermute | solution.py:166
  2.8 4.7 %collective-permute-start.1 = (bf16[32,1024]{1,0:T(8,128)(2,1)}, bf16[32,1024]{1,0:T(8,128)(2,1)S(1)}, u32[]{:S(2)}, u32[]{:S(2)}) collective-permute-start(bf16[32,1024]{1,0:T(8,128)(2,1)} %bitcast.97), channel_id=1, source_target_pairs={{0,16},{16,0},{1,17},{17,1},{2,18},{18,2},{3,19},{19,3},{4,20},{20... | collective-permute-start | bytes 196616 | tf_op jit(solution)/shard_map/ppermute | solution.py:166
  7.5 7.0 %copy-start.24 = (bf16[1,32,1024]{2,1,0:T(8,128)(2,1)S(1)}, bf16[1,32,1024]{2,1,0:T(8,128)(2,1)}, u32[]{:S(2)}) copy-start(bf16[1,32,1024]{2,1,0:T(8,128)(2,1)} %param.10) | copy-start | bytes 196612
  7.5 7.0 %copy-start.25 = (bf16[1,32,1024]{2,1,0:T(8,128)(2,1)S(1)}, bf16[1,32,1024]{2,1,0:T(8,128)(2,1)}, u32[]{:S(2)}) copy-start(bf16[1,32,1024]{2,1,0:T(8,128)(2,1)} %param.11) | copy-start | bytes 196612
  7.5 58.1 %all-to-all-start = ((bf16[8,2,128,1024]{3,2,1,0:T(8,128)(2,1)}), bf16[8,2,128,1024]{3,2,1,0:T(8,128)(2,1)}, u32[]{:S(2)}, u32[]{:S(2)}) async-start(bf16[8,2,128,1024]{3,2,1,0:T(8,128)(2,1)} %shard_map.94), calls=%async_computation | async-start | bytes 8388608 | tf_op jit(solution)/shard_map/all_to_all | solution.py:185
  14.6 31.6 %copy-start.16 = (bf16[2,2,32,1024]{3,2,1,0:T(8,128)(2,1)}, bf16[2,2,32,1024]{3,2,1,0:T(8,128)(2,1)S(1)}, u32[]{:S(2)}) copy-start(bf16[2,2,32,1024]{3,2,1,0:T(8,128)(2,1)S(1)} %pad_maximum_fusion.refs_0_) | copy-start | bytes 786436
  14.6 10.9 %collective-permute-start.2 = (bf16[2,2,32,1024]{3,2,1,0:T(8,128)(2,1)S(1)}, bf16[2,2,32,1024]{3,2,1,0:T(8,128)(2,1)S(1)}, u32[]{:S(2)}, u32[]{:S(2)}) collective-permute-start(bf16[2,2,32,1024]{3,2,1,0:T(8,128)(2,1)S(1)} %pad_maximum_fusion.refs_0_), channel_id=1, source_target_pairs={{0,32},{32,64},{64,96},{96,128},{128,160},{160,192},{192,224},{224... | collective-permute-start | bytes 786440 | tf_op jit(solution)/shard_map/ppermute | solution.py:179
  16.3 9.2 %collective-permute-start.6 = (bf16[2,2,32,1024]{3,2,1,0:T(8,128)(2,1)S(1)}, bf16[2,2,32,1024]{3,2,1,0:T(8,128)(2,1)S(1)}, u32[]{:S(2)}, u32[]{:S(2)}) collective-permute-start(bf16[2,2,32,1024]{3,2,1,0:T(8,128)(2,1)S(1)} %pad_maximum_fusion.refs_0_), channel_id=1, source_target_pairs={{0,224},{32,0},{64,32},{96,64},{128,96},{160,128},{192,160},{224,1... | collective-permute-start | bytes 786440 | tf_op jit(solution)/shard_map/ppermute | solution.py:181
  25.4 20.7 %copy-start.17 = (bf16[2,2,32,1024]{3,2,1,0:T(8,128)(2,1)}, bf16[2,2,32,1024]{3,2,1,0:T(8,128)(2,1)S(1)}, u32[]{:S(2)}) copy-start(bf16[2,2,32,1024]{3,2,1,0:T(8,128)(2,1)S(1)} %collective-permute-done.2.refs_1_) | copy-start | bytes 786436
  25.4 7.1 %collective-permute-start.3 = (bf16[2,2,32,1024]{3,2,1,0:T(8,128)(2,1)S(1)}, bf16[2,2,32,1024]{3,2,1,0:T(8,128)(2,1)S(1)}, u32[]{:S(2)}, u32[]{:S(2)}) collective-permute-start(bf16[2,2,32,1024]{3,2,1,0:T(8,128)(2,1)S(1)} %collective-permute-done.2.refs_1_), channel_id=1, source_target_pairs={{0,32},{32,64},{64,96},{96,128},{128,160},{160,192},{192,224},{224... | collective-permute-start | bytes 786440 | tf_op jit(solution)/shard_map/ppermute | solution.py:179
  25.5 20.7 %copy-start.18 = (bf16[2,2,32,1024]{3,2,1,0:T(8,128)(2,1)}, bf16[2,2,32,1024]{3,2,1,0:T(8,128)(2,1)S(1)}, u32[]{:S(2)}) copy-start(bf16[2,2,32,1024]{3,2,1,0:T(8,128)(2,1)S(1)} %collective-permute-done.6.refs_7_) | copy-start | bytes 786436
  25.5 7.0 %collective-permute-start.7 = (bf16[2,2,32,1024]{3,2,1,0:T(8,128)(2,1)S(1)}, bf16[2,2,32,1024]{3,2,1,0:T(8,128)(2,1)S(1)}, u32[]{:S(2)}, u32[]{:S(2)}) collective-permute-start(bf16[2,2,32,1024]{3,2,1,0:T(8,128)(2,1)S(1)} %collective-permute-done.6.refs_7_), channel_id=1, source_target_pairs={{0,224},{32,0},{64,32},{96,64},{128,96},{160,128},{192,160},{224,1... | collective-permute-start | bytes 786440 | tf_op jit(solution)/shard_map/ppermute | solution.py:181
  32.5 13.7 %copy-start.19 = (bf16[2,2,32,1024]{3,2,1,0:T(8,128)(2,1)}, bf16[2,2,32,1024]{3,2,1,0:T(8,128)(2,1)S(1)}, u32[]{:S(2)}) copy-start(bf16[2,2,32,1024]{3,2,1,0:T(8,128)(2,1)S(1)} %collective-permute-done.3.refs_2_) | copy-start | bytes 786436
  32.5 6.8 %collective-permute-start.4 = (bf16[2,2,32,1024]{3,2,1,0:T(8,128)(2,1)S(1)}, bf16[2,2,32,1024]{3,2,1,0:T(8,128)(2,1)S(1)}, u32[]{:S(2)}, u32[]{:S(2)}) collective-permute-start(bf16[2,2,32,1024]{3,2,1,0:T(8,128)(2,1)S(1)} %collective-permute-done.3.refs_2_), channel_id=1, source_target_pairs={{0,32},{32,64},{64,96},{96,128},{128,160},{160,192},{192,224},{224... | collective-permute-start | bytes 786440 | tf_op jit(solution)/shard_map/ppermute | solution.py:179
  32.5 13.7 %copy-start.20 = (bf16[2,2,32,1024]{3,2,1,0:T(8,128)(2,1)}, bf16[2,2,32,1024]{3,2,1,0:T(8,128)(2,1)S(1)}, u32[]{:S(2)}) copy-start(bf16[2,2,32,1024]{3,2,1,0:T(8,128)(2,1)S(1)} %collective-permute-done.7.refs_6_) | copy-start | bytes 786436
  32.5 7.4 %collective-permute-start.8 = (bf16[2,2,32,1024]{3,2,1,0:T(8,128)(2,1)S(1)}, bf16[2,2,32,1024]{3,2,1,0:T(8,128)(2,1)S(1)}, u32[]{:S(2)}, u32[]{:S(2)}) collective-permute-start(bf16[2,2,32,1024]{3,2,1,0:T(8,128)(2,1)S(1)} %collective-permute-done.7.refs_6_), channel_id=1, source_target_pairs={{0,224},{32,0},{64,32},{96,64},{128,96},{160,128},{192,160},{224,1... | collective-permute-start | bytes 786440 | tf_op jit(solution)/shard_map/ppermute | solution.py:181
  39.3 6.9 %copy-start.21 = (bf16[2,2,32,1024]{3,2,1,0:T(8,128)(2,1)}, bf16[2,2,32,1024]{3,2,1,0:T(8,128)(2,1)S(1)}, u32[]{:S(2)}) copy-start(bf16[2,2,32,1024]{3,2,1,0:T(8,128)(2,1)S(1)} %collective-permute-done.4.refs_3_) | copy-start | bytes 786436
  39.3 6.8 %collective-permute-start.5 = (bf16[2,2,32,1024]{3,2,1,0:T(8,128)(2,1)S(1)}, bf16[2,2,32,1024]{3,2,1,0:T(8,128)(2,1)S(1)}, u32[]{:S(2)}, u32[]{:S(2)}) collective-permute-start(bf16[2,2,32,1024]{3,2,1,0:T(8,128)(2,1)S(1)} %collective-permute-done.4.refs_3_), channel_id=1, source_target_pairs={{0,32},{32,64},{64,96},{96,128},{128,160},{160,192},{192,224},{224... | collective-permute-start | bytes 786440 | tf_op jit(solution)/shard_map/ppermute | solution.py:179
  39.9 6.3 %copy-start.22 = (bf16[2,2,32,1024]{3,2,1,0:T(8,128)(2,1)}, bf16[2,2,32,1024]{3,2,1,0:T(8,128)(2,1)S(1)}, u32[]{:S(2)}) copy-start(bf16[2,2,32,1024]{3,2,1,0:T(8,128)(2,1)S(1)} %collective-permute-done.8.refs_5_) | copy-start | bytes 786436
  50.6 8.5 %collective-permute-start.9 = (bf16[8,2,2,32,1024]{4,3,2,1,0:T(8,128)(2,1)}, bf16[8,2,2,32,1024]{4,3,2,1,0:T(8,128)(2,1)S(1)}, u32[]{:S(2)}, u32[]{:S(2)}) collective-permute-start(bf16[8,2,2,32,1024]{4,3,2,1,0:T(8,128)(2,1)} %shard_map.95.mine), channel_id=1, source_target_pairs={{0,8},{8,0},{1,9},{9,1},{2,10},{10,2},{3,11},{11,3},{4,12},{12,4},... | collective-permute-start | bytes 6291464 | tf_op jit(solution)/shard_map/ppermute | solution.py:166
  60.5 1.6 copy-start.1
  65.6 2.9 %copy-start.7 = (bf16[8,2,2,32,1024]{4,3,2,1,0:T(8,128)(2,1)S(1)}, bf16[8,2,2,32,1024]{4,3,2,1,0:T(8,128)(2,1)}, u32[]{:S(2)}) copy-start(bf16[8,2,2,32,1024]{4,3,2,1,0:T(8,128)(2,1)} %copy-done.6) | copy-start | bytes 6291460
  68.5 2.4 %copy-start.14 = (bf16[8,1,128,1024]{3,2,1,0:T(8,128)(2,1)}, bf16[8,1,128,1024]{3,2,1,0:T(8,128)(2,1)S(1)}, u32[]{:S(2)}) copy-start(bf16[8,1,128,1024]{3,2,1,0:T(8,128)(2,1)S(1)} %get-tuple-element.32) | copy-start | bytes 6291460
  68.5 2.4 %copy-start.8 = (bf16[8,1,128,1024]{3,2,1,0:T(8,128)(2,1)}, bf16[8,1,128,1024]{3,2,1,0:T(8,128)(2,1)S(1)}, u32[]{:S(2)}) copy-start(bf16[8,1,128,1024]{3,2,1,0:T(8,128)(2,1)S(1)} %get-tuple-element.31) | copy-start | bytes 6291460
  72.2 3.8 %collective-permute-start.10 = (bf16[512,1024]{1,0:T(8,128)(2,1)S(1)}, bf16[512,1024]{1,0:T(8,128)(2,1)}, u32[]{:S(2)}, u32[]{:S(2)}) collective-permute-start(bf16[512,1024]{1,0:T(8,128)(2,1)S(1)} %convolution_convert_fusion.1), channel_id=1, source_target_pairs={{0,8},{8,0},{1,9},{9,1},{2,10},{10,2},{3,11},{11,3},{4,12},{12,4},... | collective-permute-start | bytes 3145736 | tf_op jit(solution)/shard_map/ppermute | solution.py:166
  78.5 32.0 %all-to-all-start.1 = ((bf16[16,32,1024]{2,1,0:T(8,128)(2,1)}), bf16[16,32,1024]{2,1,0:T(8,128)(2,1)S(1)}, u32[]{:S(2)}, u32[]{:S(2)}) async-start(bf16[16,32,1024]{2,1,0:T(8,128)(2,1)} %bitcast.87), calls=%async_computation.1 | async-start | bytes 2097152 | tf_op jit(solution)/shard_map/all_to_all | solution.py:216
  89.9 5.5 %copy-start.10 = (f32[1024,1024]{1,0:T(8,128)}, f32[1024,1024]{1,0:T(8,128)S(1)}, u32[]{:S(2)}) copy-start(f32[1024,1024]{1,0:T(8,128)S(1)} %convolution_multiply_fusion) | copy-start | bytes 12582916
  89.9 3.1 %copy-start.15 = (bf16[8,1,128,1024]{3,2,1,0:T(8,128)(2,1)S(1)}, bf16[8,1,128,1024]{3,2,1,0:T(8,128)(2,1)}, u32[]{:S(2)}) copy-start(bf16[8,1,128,1024]{3,2,1,0:T(8,128)(2,1)} %copy-done.14) | copy-start | bytes 6291460
  91.1 7.9 %collective-permute-start.12 = (bf16[8,2,32,1024]{3,2,1,0:T(8,128)(2,1)}, bf16[8,2,32,1024]{3,2,1,0:T(8,128)(2,1)}, u32[]{:S(2)}, u32[]{:S(2)}) collective-permute-start(bf16[8,2,32,1024]{3,2,1,0:T(8,128)(2,1)} %fusion.3), channel_id=1, source_target_pairs={{0,8},{8,0},{1,9},{9,1},{2,10},{10,2},{3,11},{11,3},{4,12},{12,4},... | collective-permute-start | bytes 3145736 | tf_op jit(solution)/shard_map/ppermute | solution.py:166
  95.4 2.0 %copy-start.11 = (f32[1024,1024]{1,0:T(8,128)}, f32[1024,1024]{1,0:T(8,128)S(1)}, u32[]{:S(2)}) copy-start(f32[1024,1024]{1,0:T(8,128)S(1)} %fusion.21) | copy-start | bytes 12582916
  98.6 3.0 %collective-permute-start.11 = (bf16[8,2,32,1024]{3,2,1,0:T(8,128)(2,1)}, bf16[8,2,32,1024]{3,2,1,0:T(8,128)(2,1)}, u32[]{:S(2)}, u32[]{:S(2)}) collective-permute-start(bf16[8,2,32,1024]{3,2,1,0:T(8,128)(2,1)} %fusion.2), channel_id=1, source_target_pairs={{0,8},{8,0},{1,9},{9,1},{2,10},{10,2},{3,11},{11,3},{4,12},{12,4},... | collective-permute-start | bytes 3145736 | tf_op jit(solution)/shard_map/ppermute | solution.py:166
  98.9 3.1 %copy-start.12 = (f32[1024,1024]{1,0:T(8,128)S(1)}, f32[1024,1024]{1,0:T(8,128)}, u32[]{:S(2)}) copy-start(f32[1024,1024]{1,0:T(8,128)} %copy-done.11) | copy-start | bytes 12582916
  105.1 29.8 %copy-start.5 = (f32[1,1024]{1,0:T(1,128)S(1)}, f32[1,1024]{1,0:T(1,128)}, u32[]{:S(2)}) copy-start(f32[1,1024]{1,0:T(1,128)} %eig_cols.1) | copy-start | bytes 12292
  105.1 31.9 %collective-permute-start.13 = (bf16[8,64,1024]{2,1,0:T(8,128)(2,1)}, bf16[8,64,1024]{2,1,0:T(8,128)(2,1)}, u32[]{:S(2)}, u32[]{:S(2)}) collective-permute-start(bf16[8,64,1024]{2,1,0:T(8,128)(2,1)} %get-tuple-element.34), channel_id=1, source_target_pairs={{0,16},{16,0},{1,17},{17,1},{2,18},{18,2},{3,19},{19,3},{4,20},{20... | collective-permute-start | bytes 3145736 | tf_op jit(solution)/shard_map/ppermute | solution.py:166
  111.4 23.5 %all-to-all-start.2 = ((bf16[8,32,1024]{2,1,0:T(8,128)(2,1)}), bf16[8,32,1024]{2,1,0:T(8,128)(2,1)S(1)}, u32[]{:S(2)}, u32[]{:S(2)}) async-start(bf16[8,32,1024]{2,1,0:T(8,128)(2,1)} %copy-done.2), calls=%async_computation.2 | async-start | bytes 1048576 | tf_op jit(solution)/shard_map/all_to_all | solution.py:217
  134.9 2.1 %copy-start.9 = (bf16[8,64,1024]{2,1,0:T(8,128)(2,1)S(1)}, bf16[8,64,1024]{2,1,0:T(8,128)(2,1)}, u32[]{:S(2)}) copy-start(bf16[8,64,1024]{2,1,0:T(8,128)(2,1)} %get-tuple-element.33) | copy-start | bytes 3145732
  136.4 3.3 %collective-permute-start.14 = (f32[64,1024]{1,0:T(8,128)S(1)}, f32[64,1024]{1,0:T(8,128)S(1)}, u32[]{:S(2)}, u32[]{:S(2)}) collective-permute-start(f32[64,1024]{1,0:T(8,128)S(1)} %dynamic-slice_bitcast_fusion), channel_id=1, source_target_pairs={{0,8},{8,0},{1,9},{9,1},{2,10},{10,2},{3,11},{11,3},{4,12},{12,4},... | collective-permute-start | bytes 786440 | tf_op jit(solution)/shard_map/ppermute | solution.py:166
  139.7 14.6 %copy-start.26 = (s32[8]{0:T(128)S(1)}, s32[8]{0:T(128)}, u32[]{:S(2)}) copy-start(s32[8]{0:T(128)} %assign.1) | copy-start | bytes 100
  139.7 32.8 %all-to-all-start.3 = ((bf16[8,64,1024]{2,1,0:T(8,128)(2,1)}), bf16[8,64,1024]{2,1,0:T(8,128)(2,1)S(1)}, u32[]{:S(2)}, u32[]{:S(2)}) async-start(bf16[8,64,1024]{2,1,0:T(8,128)(2,1)} %add_convert_fusion), calls=%async_computation.3 | async-start | bytes 2097152 | tf_op jit(solution)/shard_map/all_to_all | solution.py:235
  143.3 5.2 %collective-permute-start.15 = (f32[32,1024]{1,0:T(8,128)S(1)}, f32[32,1024]{1,0:T(8,128)S(1)}, u32[]{:S(2)}, u32[]{:S(2)}) collective-permute-start(f32[32,1024]{1,0:T(8,128)S(1)} %dynamic-slice_bitcast_fusion.1), channel_id=1, source_target_pairs={{0,16},{16,0},{1,17},{17,1},{2,18},{18,2},{3,19},{19,3},{4,20},{20... | collective-permute-start | bytes 393224 | tf_op jit(solution)/shard_map/ppermute | solution.py:166
  148.5 11.2 %collective-permute-start.16 = (bf16[32,1024]{1,0:T(8,128)(2,1)S(1)}, bf16[32,1024]{1,0:T(8,128)(2,1)S(1)}, u32[]{:S(2)}, u32[]{:S(2)}) collective-permute-start(bf16[32,1024]{1,0:T(8,128)(2,1)S(1)} %fusion.10), channel_id=1, source_target_pairs={{0,7},{1,4},{2,5},{3,6},{4,3},{5,0},{6,1},{7,2},{8,15},{9,12},{10,... | collective-permute-start | bytes 196616 | tf_op jit(solution)/shard_map/ppermute | solution.py:248
  152.9 8.3 %collective-permute-start.17 = (bf16[32,1024]{1,0:T(8,128)(2,1)S(1)}, bf16[32,1024]{1,0:T(8,128)(2,1)S(1)}, u32[]{:S(2)}, u32[]{:S(2)}) collective-permute-start(bf16[32,1024]{1,0:T(8,128)(2,1)S(1)} %fusion.10), channel_id=1, source_target_pairs={{0,6},{1,7},{2,4},{3,5},{4,2},{5,3},{6,0},{7,1},{8,14},{9,15},{10,... | collective-permute-start | bytes 196616 | tf_op jit(solution)/shard_map/ppermute | solution.py:248
  154.3 7.7 %collective-permute-start.18 = (bf16[32,1024]{1,0:T(8,128)(2,1)S(1)}, bf16[32,1024]{1,0:T(8,128)(2,1)S(1)}, u32[]{:S(2)}, u32[]{:S(2)}) collective-permute-start(bf16[32,1024]{1,0:T(8,128)(2,1)S(1)} %fusion.10), channel_id=1, source_target_pairs={{0,5},{1,6},{2,7},{3,4},{4,1},{5,2},{6,3},{7,0},{8,13},{9,14},{10,... | collective-permute-start | bytes 196616 | tf_op jit(solution)/shard_map/ppermute | solution.py:248
  156.5 5.4 %collective-permute-start.19 = (bf16[32,1024]{1,0:T(8,128)(2,1)S(1)}, bf16[32,1024]{1,0:T(8,128)(2,1)S(1)}, u32[]{:S(2)}, u32[]{:S(2)}) collective-permute-start(bf16[32,1024]{1,0:T(8,128)(2,1)S(1)} %fusion.10), channel_id=1, source_target_pairs={{0,4},{1,5},{2,6},{3,7},{4,0},{5,1},{6,2},{7,3},{8,12},{9,13},{10,... | collective-permute-start | bytes 196616 | tf_op jit(solution)/shard_map/ppermute | solution.py:248
  157.5 4.4 %collective-permute-start.20 = (bf16[32,1024]{1,0:T(8,128)(2,1)S(1)}, bf16[32,1024]{1,0:T(8,128)(2,1)S(1)}, u32[]{:S(2)}, u32[]{:S(2)}) collective-permute-start(bf16[32,1024]{1,0:T(8,128)(2,1)S(1)} %fusion.10), channel_id=1, source_target_pairs={{0,3},{1,0},{2,1},{3,2},{4,7},{5,4},{6,5},{7,6},{8,11},{9,8},{10,9... | collective-permute-start | bytes 196616 | tf_op jit(solution)/shard_map/ppermute | solution.py:248
  159.7 4.6 %collective-permute-start.21 = (bf16[32,1024]{1,0:T(8,128)(2,1)S(1)}, bf16[32,1024]{1,0:T(8,128)(2,1)S(1)}, u32[]{:S(2)}, u32[]{:S(2)}) collective-permute-start(bf16[32,1024]{1,0:T(8,128)(2,1)S(1)} %fusion.10), channel_id=1, source_target_pairs={{0,2},{1,3},{2,0},{3,1},{4,6},{5,7},{6,4},{7,5},{8,10},{9,11},{10,... | collective-permute-start | bytes 196616 | tf_op jit(solution)/shard_map/ppermute | solution.py:248
  161.2 4.3 %collective-permute-start.22 = (bf16[32,1024]{1,0:T(8,128)(2,1)S(1)}, bf16[32,1024]{1,0:T(8,128)(2,1)S(1)}, u32[]{:S(2)}, u32[]{:S(2)}) collective-permute-start(bf16[32,1024]{1,0:T(8,128)(2,1)S(1)} %fusion.10), channel_id=1, source_target_pairs={{0,1},{1,2},{2,3},{3,0},{4,5},{5,6},{6,7},{7,4},{8,9},{9,10},{10,1... | collective-permute-start | bytes 196616 | tf_op jit(solution)/shard_map/ppermute | solution.py:248
  (6 other events, 7.2 us)

commit v2 on v1

--- a/solution.py
+++ b/solution.py
@@ -215,6 +215,7 @@
     halves = (keep.astype(f32) + give.astype(f32)).astype(bf16)
     spread = spread_sum(lax.all_to_all(pair, ("xl", "z"), 0, 0, tiled=True), n_z)
     rotated = lax.all_to_all(spread, "z", 0, 0, tiled=True).reshape(n_z * rows, width)
+    halves, _ = lax.optimization_barrier((halves, rotated))
 
     quarter = n_z * rows
     first = (core * n_xl + xl) * quarter
@@ -231,7 +232,6 @@
         return keep + swap(give, axis)
 
     result = fold(result, "core", core)
-    halves, result = lax.optimization_barrier((halves, result))
     sums = jnp.sum(lax.all_to_all(halves, "z", 0, 0, tiled=True).astype(f32), axis=0)
     factor_g, factor_a = sums[:rows], sums[rows:]
     result = fold(result, "xl", xl).astype(bf16)

time: 174 us -> 174 us (level)
  waiting for transfers between devices: 58.9 us -> 54.1 us
  starting transfers between devices: 58 us -> 60.1 us
    all_to_all x1, waiting for transfers between devices: 16.9 us -> 0.15 us  [body(): lax.all_to_all(spread, 'z', 0, 0, tiled=True).reshape(n_z * rows, width)]
    ppermute x9, waiting for transfers between devices: 8.2 us -> 24.3 us  [swap(): return lax.ppermute(x, axis, [(0, 1), (1, 0)])]
    all_to_all x1, waiting for transfers between devices: 5.8 us -> 1.24 us  [body(): lax.all_to_all(halves, 'z', 0, 0, tiled=True).astype(f32)]
    all_to_all x1, starting transfers between devices: 3.57 us -> 5.79 us  [body(): lax.all_to_all(halves, 'z', 0, 0, tiled=True).astype(f32)]
    unnamed x54 -> x52, local copies, waits for them, and re-layouts: 11.7 us -> 11.6 us
  transfers between devices with their start and end apart: 27 -> 27, of which waited for: 13 -> 15; matrix products, arithmetic and copies ran while one was open for 14% -> 14% of each run, Pallas kernels for 6% -> 6%
where the time goes in v2:
time: 174 us; the launch traced here: 172 us
  starting transfers between devices  60.1 us (35%)
  waiting for transfers between devices  54.1 us (31%)
  local copies, waits for them, and re-layouts  18.5 us (11%)
  other arithmetic  14.3 us (8%)
  matrix products  13.8 us (8%)
  Pallas kernels  10.4 us (6%)
    ppermute x9, waiting for transfers between devices, swap(): return lax.ppermute(x, axis, [(0, 1), (1, 0)])  24.3 us
    ppermute x4, waiting for transfers between devices, body(): lax.ppermute(up, 'z', [(i, (i + 1) % n_z) for i in range(n_z)])  19.9 us
    ppermute x7, starting transfers between devices, body(): pieces[s] = lax.ppermute(result, GRP, moves)  12.6 us
    unnamed x52, local copies, waits for them, and re-layouts  11.6 us
    dot_general x4, matrix products, dot_first(): return lax.dot_general(x, y, contract_first, preferred_element_type=f32)  11.4 us
    ppermute x9, starting transfers between devices, swap(): return lax.ppermute(x, axis, [(0, 1), (1, 0)])  11.3 us
    ppermute x3, starting transfers between devices, body(): lax.ppermute(down, 'z', [(i, (i - 1) % n_z) for i in range(n_z)])  9.35 us
    all_to_all x1, starting transfers between devices, body(): own = lax.all_to_all(send, GRP, 0, 0, tiled=True)  6.95 us
  transfers between devices with their start and end apart: 27, of which 15 were waited for; matrix products, arithmetic and copies ran while one was open for 14% of the time, Pallas kernels for 6%

profile of v2, /device:TPU:1, one launch (start us, length us, event | category | flops | bytes accessed | tf_op | source)
XLA Modules:
  0.0 172.2 jit_solution(9387954642571259298)
XLA Ops:
  0.6 2.1 %collective-permute-start = (bf16[32,1024]{1,0:T(8,128)(2,1)}, bf16[32,1024]{1,0:T(8,128)(2,1)S(1)}, u32[]{:S(2)}, u32[]{:S(2)}) collective-permute-start(bf16[32,1024]{1,0:T(8,128)(2,1)} %bitcast.98), channel_id=1, source_target_pairs={{0,16},{16,0},{1,17},{17,1},{2,18},{18,2},{3,19},{19,3},{4,20},{20... | collective-permute-start | bytes 196616 | tf_op jit(solution)/shard_map/ppermute | solution.py:166
  2.9 4.6 %shard_map.94 = bf16[8,2,128,1024]{3,2,1,0:T(8,128)(2,1)} custom-call(s32[8]{0:T(128)} %assign.1, bf16[8,128,1024]{2,1,0:T(8,128)(2,1)} %grads.1, bf16[8,128,1024]{2,1,0:T(8,128)(2,1)} %acts.1), custom_call_target="tpu_custom_call" | custom-call | bytes 8388608 | tf_op jit(solution)/shard_map/pallas_call | solution.py:38
  7.5 6.9 %all-to-all-start = ((bf16[8,2,128,1024]{3,2,1,0:T(8,128)(2,1)}), bf16[8,2,128,1024]{3,2,1,0:T(8,128)(2,1)}, u32[]{:S(2)}, u32[]{:S(2)}) async-start(bf16[8,2,128,1024]{3,2,1,0:T(8,128)(2,1)} %shard_map.94), calls=%async_computation | async-start | bytes 8388608 | tf_op jit(solution)/shard_map/all_to_all | solution.py:185
  14.6 1.7 collective-permute-start.2
  16.3 4.0 %collective-permute-start.6 = (bf16[2,2,32,1024]{3,2,1,0:T(8,128)(2,1)S(1)}, bf16[2,2,32,1024]{3,2,1,0:T(8,128)(2,1)S(1)}, u32[]{:S(2)}, u32[]{:S(2)}) collective-permute-start(bf16[2,2,32,1024]{3,2,1,0:T(8,128)(2,1)S(1)} %pad_maximum_fusion.refs_0_), channel_id=1, source_target_pairs={{0,224},{32,0},{64,32},{96,64},{128,96},{160,128},{192,160},{224,1... | collective-permute-start | bytes 786440 | tf_op jit(solution)/shard_map/ppermute | solution.py:181
  20.3 5.1 %collective-permute-done.2.refs_1_ = bf16[2,2,32,1024]{3,2,1,0:T(8,128)(2,1)S(1)} collective-permute-done((bf16[2,2,32,1024]{3,2,1,0:T(8,128)(2,1)S(1)}, bf16[2,2,32,1024]{3,2,1,0:T(8,128)(2,1)S(1)}, u32[]{:S(2)}, u32[]{:S(2)}) %collective-permute-start.2) | collective-permute-done | bytes 262176 | tf_op jit(solution)/shard_map/ppermute | solution.py:179
  25.5 2.7 %collective-permute-start.7 = (bf16[2,2,32,1024]{3,2,1,0:T(8,128)(2,1)S(1)}, bf16[2,2,32,1024]{3,2,1,0:T(8,128)(2,1)S(1)}, u32[]{:S(2)}, u32[]{:S(2)}) collective-permute-start(bf16[2,2,32,1024]{3,2,1,0:T(8,128)(2,1)S(1)} %collective-permute-done.6.refs_7_), channel_id=1, source_target_pairs={{0,224},{32,0},{64,32},{96,64},{128,96},{160,128},{192,160},{224,1... | collective-permute-start | bytes 786440 | tf_op jit(solution)/shard_map/ppermute | solution.py:181
  28.1 4.4 %collective-permute-done.3.refs_2_ = bf16[2,2,32,1024]{3,2,1,0:T(8,128)(2,1)S(1)} collective-permute-done((bf16[2,2,32,1024]{3,2,1,0:T(8,128)(2,1)S(1)}, bf16[2,2,32,1024]{3,2,1,0:T(8,128)(2,1)S(1)}, u32[]{:S(2)}, u32[]{:S(2)}) %collective-permute-start.3) | collective-permute-done | bytes 262176 | tf_op jit(solution)/shard_map/ppermute | solution.py:179
  32.5 2.7 %collective-permute-start.8 = (bf16[2,2,32,1024]{3,2,1,0:T(8,128)(2,1)S(1)}, bf16[2,2,32,1024]{3,2,1,0:T(8,128)(2,1)S(1)}, u32[]{:S(2)}, u32[]{:S(2)}) collective-permute-start(bf16[2,2,32,1024]{3,2,1,0:T(8,128)(2,1)S(1)} %collective-permute-done.7.refs_6_), channel_id=1, source_target_pairs={{0,224},{32,0},{64,32},{96,64},{128,96},{160,128},{192,160},{224,1... | collective-permute-start | bytes 786440 | tf_op jit(solution)/shard_map/ppermute | solution.py:181
  35.2 4.2 %collective-permute-done.4.refs_3_ = bf16[2,2,32,1024]{3,2,1,0:T(8,128)(2,1)S(1)} collective-permute-done((bf16[2,2,32,1024]{3,2,1,0:T(8,128)(2,1)S(1)}, bf16[2,2,32,1024]{3,2,1,0:T(8,128)(2,1)S(1)}, u32[]{:S(2)}, u32[]{:S(2)}) %collective-permute-start.4) | collective-permute-done | bytes 262176 | tf_op jit(solution)/shard_map/ppermute | solution.py:179
  39.9 6.3 %collective-permute-done.5.refs_4_ = bf16[2,2,32,1024]{3,2,1,0:T(8,128)(2,1)S(1)} collective-permute-done((bf16[2,2,32,1024]{3,2,1,0:T(8,128)(2,1)S(1)}, bf16[2,2,32,1024]{3,2,1,0:T(8,128)(2,1)S(1)}, u32[]{:S(2)}, u32[]{:S(2)}) %collective-permute-start.5) | collective-permute-done | bytes 262176 | tf_op jit(solution)/shard_map/ppermute | solution.py:179
  46.9 3.6 %shard_map.95.mine = bf16[8,2,2,32,1024]{4,3,2,1,0:T(8,128)(2,1)} custom-call(s32[8]{0:T(128)} %compare_select_fusion.4.index, bf16[2,2,32,1024]{3,2,1,0:T(8,128)(2,1)} %copy-done.15, bf16[2,2,32,1024]{3,2,1,0:T(8,128)(2,1)} %copy-done.16, bf16[2,2,32,1024]{3,2,1,0:T(8,128)(2,1)} %copy-done.18, bf16[2,2,32,1024]{3,2,1,0:T(8,128)(2,1)} %copy-done.20, ...), custom_call_target="tpu_custom_call" | custom-call | tf_op jit(solution)/shard_map/pallas_call | solution.py:70
  50.5 4.5 %collective-permute-start.9 = (bf16[8,2,2,32,1024]{4,3,2,1,0:T(8,128)(2,1)}, bf16[8,2,2,32,1024]{4,3,2,1,0:T(8,128)(2,1)S(1)}, u32[]{:S(2)}, u32[]{:S(2)}) collective-permute-start(bf16[8,2,2,32,1024]{4,3,2,1,0:T(8,128)(2,1)} %shard_map.95.mine), channel_id=1, source_target_pairs={{0,8},{8,0},{1,9},{9,1},{2,10},{10,2},{3,11},{11,3},{4,12},{12,4},... | collective-permute-start | bytes 6291464 | tf_op jit(solution)/shard_map/ppermute | solution.py:166
  55.0 4.0 %collective-permute-done.9.other = bf16[8,2,2,32,1024]{4,3,2,1,0:T(8,128)(2,1)S(1)} collective-permute-done((bf16[8,2,2,32,1024]{4,3,2,1,0:T(8,128)(2,1)}, bf16[8,2,2,32,1024]{4,3,2,1,0:T(8,128)(2,1)S(1)}, u32[]{:S(2)}, u32[]{:S(2)}) %collective-permute-start.9) | collective-permute-done | bytes 2097184 | tf_op jit(solution)/shard_map/ppermute | solution.py:166
  59.0 1.4 copy-done.3
  60.4 1.6 copy-done.1
  62.0 1.6 copy-done.4
  64.2 1.3 copy-done.6
  65.5 2.8 %fusion.20 = (bf16[8,1,128,1024]{3,2,1,0:T(8,128)(2,1)S(1)}, bf16[8,1,128,1024]{3,2,1,0:T(8,128)(2,1)S(1)}) fusion(bf16[8,2,128,1024]{3,2,1,0:T(8,128)(2,1)} %all-to-all-done), kind=kLoop, calls=%fused_computation.66 | loop fusion | bytes 8388608 | tf_op jit(solution)/shard_map/slice | solution.py:188
  68.4 2.3 %convolution_convert_fusion = bf16[1024,1024]{1,0:T(8,128)(2,1)S(1)} fusion(bf16[1024,1024]{1,0:T(8,128)(2,1)S(1)} %bitcast.92, bf16[1024,1024]{1,0:T(8,128)(2,1)S(1)} %bitcast.83), kind=kOutput, calls=%fused_computation.14 | convolution fusion | flops 2148532224 | bytes 6291456 | tf_op jit(solution)/shard_map/dot_general | solution.py:201
  70.8 1.3 convolution_convert_fusion.1
  72.8 3.2 %convolution_convert_fusion.2 = bf16[512,1024]{1,0:T(8,128)(2,1)S(1)} fusion(bf16[1024,1024]{1,0:T(8,128)(2,1)} %bitcast.85, bf16[1024,1024]{1,0:T(8,128)(2,1)} %copy-done.12, s32[]{:T(128)S(6)} %select_n.87), kind=kOutput, calls=%fused_computation.16 | convolution fusion | flops 1074266112 | bytes 4194308 | tf_op jit(solution)/shard_map/dot_general | solution.py:191
  76.0 2.5 %add_convert_fusion.1 = bf16[512,1024]{1,0:T(8,128)(2,1)} fusion(bf16[512,1024]{1,0:T(8,128)(2,1)} %collective-permute-done.10, bf16[512,1024]{1,0:T(8,128)(2,1)S(1)} %convolution_convert_fusion.2), kind=kLoop, calls=%fused_computation.13 | loop fusion | flops 2097152 | bytes 3145728 | tf_op jit(solution)/shard_map/convert_element_type | solution.py:207
  78.5 6.8 %all-to-all-start.1 = ((bf16[16,32,1024]{2,1,0:T(8,128)(2,1)}), bf16[16,32,1024]{2,1,0:T(8,128)(2,1)S(1)}, u32[]{:S(2)}, u32[]{:S(2)}) async-start(bf16[16,32,1024]{2,1,0:T(8,128)(2,1)} %bitcast.87), calls=%async_computation.1 | async-start | bytes 2097152 | tf_op jit(solution)/shard_map/all_to_all | solution.py:216
  85.3 4.6 %convolution_multiply_fusion = f32[1024,1024]{1,0:T(8,128)S(1)} fusion(bf16[1024,1024]{1,0:T(8,128)(2,1)} %bitcast.86), kind=kOutput, calls=%fused_computation.4 | convolution fusion | flops 2148532224 | bytes 6291456 | tf_op jit(solution)/shard_map/dot_general | solution.py:191
  91.3 1.7 copy-done.14
  93.0 2.4 %fusion.21 = f32[1024,1024]{1,0:T(8,128)S(1)} fusion(bf16[1024,1024]{1,0:T(8,128)(2,1)S(1)} %bitcast.93), kind=kOutput, calls=%fused_computation.67 | convolution fusion | flops 2147483648 | bytes 6291456 | tf_op jit(solution)/shard_map/dot_general | solution.py:191
  95.4 2.0 %copy-done.10 = f32[1024,1024]{1,0:T(8,128)} copy-done((f32[1024,1024]{1,0:T(8,128)}, f32[1024,1024]{1,0:T(8,128)S(1)}, u32[]{:S(2)}) %copy-start.10) | copy-done | bytes 4194328
  98.9 2.4 %fusion = bf16[8,2,32,1024]{3,2,1,0:T(8,128)(2,1)S(1)} fusion(bf16[8,2,32,1024]{3,2,1,0:T(8,128)(2,1)} %collective-permute-done.12, f32[8,2,2,32,1024]{4,3,2,1,0:T(8,128)} %bitcast.89, s32[]{:T(128)S(6)} %select_n.89), kind=kLoop, calls=%fused_computation.7 | loop fusion | flops 1572864 | bytes 4194308 | tf_op jit(solution)/shard_map/convert_element_type | solution.py:196
  102.0 1.6 fusion.1
  103.6 1.5 fusion.7
  105.1 1.6 collective-permute-start.13
  106.8 3.7 %all-to-all-done.1.src = bf16[16,32,1024]{2,1,0:T(8,128)(2,1)S(1)} async-done(((bf16[16,32,1024]{2,1,0:T(8,128)(2,1)}), bf16[16,32,1024]{2,1,0:T(8,128)(2,1)S(1)}, u32[]{:S(2)}, u32[]{:S(2)}) %all-to-all-start.1) | async-done | bytes 1048608 | tf_op jit(solution)/shard_map/all_to_all | solution.py:216
  111.4 5.5 %all-to-all-start.2 = ((bf16[8,32,1024]{2,1,0:T(8,128)(2,1)}), bf16[8,32,1024]{2,1,0:T(8,128)(2,1)S(1)}, u32[]{:S(2)}, u32[]{:S(2)}) async-start(bf16[8,32,1024]{2,1,0:T(8,128)(2,1)} %copy-done.2), calls=%async_computation.2 | async-start | bytes 1048576 | tf_op jit(solution)/shard_map/all_to_all | solution.py:217
  117.0 14.8 %collective-permute-done.13 = bf16[8,64,1024]{2,1,0:T(8,128)(2,1)} collective-permute-done((bf16[8,64,1024]{2,1,0:T(8,128)(2,1)}, bf16[8,64,1024]{2,1,0:T(8,128)(2,1)}, u32[]{:S(2)}, u32[]{:S(2)}) %collective-permute-start.13) | collective-permute-done | bytes 1048608 | tf_op jit(solution)/shard_map/ppermute | solution.py:166
  131.8 3.0 %add_convert_fusion = bf16[8,64,1024]{2,1,0:T(8,128)(2,1)} fusion(bf16[8,64,1024]{2,1,0:T(8,128)(2,1)} %collective-permute-done.13, bf16[8,64,1024]{2,1,0:T(8,128)(2,1)} %get-tuple-element.31), kind=kLoop, calls=%fused_computation.11 | loop fusion | flops 2097152 | bytes 3145728 | tf_op jit(solution)/shard_map/convert_element_type | solution.py:215
  134.9 5.8 %all-to-all-start.3 = ((bf16[8,64,1024]{2,1,0:T(8,128)(2,1)}), bf16[8,64,1024]{2,1,0:T(8,128)(2,1)}, u32[]{:S(2)}, u32[]{:S(2)}) async-start(bf16[8,64,1024]{2,1,0:T(8,128)(2,1)} %add_convert_fusion), calls=%async_computation.3 | async-start | bytes 2097152 | tf_op jit(solution)/shard_map/all_to_all | solution.py:235
  141.8 1.4 shard_map.98
  146.2 4.0 %collective-permute-done.15 = f32[32,1024]{1,0:T(8,128)S(1)} collective-permute-done((f32[32,1024]{1,0:T(8,128)S(1)}, f32[32,1024]{1,0:T(8,128)S(1)}, u32[]{:S(2)}, u32[]{:S(2)}) %collective-permute-start.15) | collective-permute-done | bytes 131104 | tf_op jit(solution)/shard_map/ppermute | solution.py:166
  150.3 4.3 %collective-permute-start.16 = (bf16[32,1024]{1,0:T(8,128)(2,1)S(1)}, bf16[32,1024]{1,0:T(8,128)(2,1)S(1)}, u32[]{:S(2)}, u32[]{:S(2)}) collective-permute-start(bf16[32,1024]{1,0:T(8,128)(2,1)S(1)} %fusion.10), channel_id=1, source_target_pairs={{0,7},{1,4},{2,5},{3,6},{4,3},{5,0},{6,1},{7,2},{8,15},{9,12},{10,... | collective-permute-start | bytes 196616 | tf_op jit(solution)/shard_map/ppermute | solution.py:248
  154.6 1.4 collective-permute-start.17
  156.0 2.2 %collective-permute-start.18 = (bf16[32,1024]{1,0:T(8,128)(2,1)S(1)}, bf16[32,1024]{1,0:T(8,128)(2,1)S(1)}, u32[]{:S(2)}, u32[]{:S(2)}) collective-permute-start(bf16[32,1024]{1,0:T(8,128)(2,1)S(1)} %fusion.10), channel_id=1, source_target_pairs={{0,5},{1,6},{2,7},{3,4},{4,1},{5,2},{6,3},{7,0},{8,13},{9,14},{10,... | collective-permute-start | bytes 196616 | tf_op jit(solution)/shard_map/ppermute | solution.py:248
  159.3 2.1 %collective-permute-start.20 = (bf16[32,1024]{1,0:T(8,128)(2,1)S(1)}, bf16[32,1024]{1,0:T(8,128)(2,1)S(1)}, u32[]{:S(2)}, u32[]{:S(2)}) collective-permute-start(bf16[32,1024]{1,0:T(8,128)(2,1)S(1)} %fusion.10), channel_id=1, source_target_pairs={{0,3},{1,0},{2,1},{3,2},{4,7},{5,4},{6,5},{7,6},{8,11},{9,8},{10,9... | collective-permute-start | bytes 196616 | tf_op jit(solution)/shard_map/ppermute | solution.py:248
  161.4 1.5 collective-permute-start.21
  163.7 2.8 %collective-permute-done.21 = bf16[32,1024]{1,0:T(8,128)(2,1)S(1)} collective-permute-done((bf16[32,1024]{1,0:T(8,128)(2,1)S(1)}, bf16[32,1024]{1,0:T(8,128)(2,1)S(1)}, u32[]{:S(2)}, u32[]{:S(2)}) %collective-permute-start.21) | collective-permute-done | bytes 65568 | tf_op jit(solution)/shard_map/ppermute | solution.py:248
  166.5 1.2 collective-permute-done.22
  168.8 1.2 all-to-all-done.3
  170.1 1.4 convert_reduce_fusion
  (94 shorter events, 15.3 us)
Async XLA Ops:
  0.6 140.1 %copy-start = (f32[1,1024]{1,0:T(1,128)S(1)}, f32[1,1024]{1,0:T(1,128)}, u32[]{:S(2)}) copy-start(f32[1,1024]{1,0:T(1,128)} %param.13) | copy-start | bytes 12292
  0.6 6.8 %collective-permute-start = (bf16[32,1024]{1,0:T(8,128)(2,1)}, bf16[32,1024]{1,0:T(8,128)(2,1)S(1)}, u32[]{:S(2)}, u32[]{:S(2)}) collective-permute-start(bf16[32,1024]{1,0:T(8,128)(2,1)} %bitcast.98), channel_id=1, source_target_pairs={{0,16},{16,0},{1,17},{17,1},{2,18},{18,2},{3,19},{19,3},{4,20},{20... | collective-permute-start | bytes 196616 | tf_op jit(solution)/shard_map/ppermute | solution.py:166
  2.8 4.7 %collective-permute-start.1 = (bf16[32,1024]{1,0:T(8,128)(2,1)}, bf16[32,1024]{1,0:T(8,128)(2,1)S(1)}, u32[]{:S(2)}, u32[]{:S(2)}) collective-permute-start(bf16[32,1024]{1,0:T(8,128)(2,1)} %bitcast.97), channel_id=1, source_target_pairs={{0,16},{16,0},{1,17},{17,1},{2,18},{18,2},{3,19},{19,3},{4,20},{20... | collective-permute-start | bytes 196616 | tf_op jit(solution)/shard_map/ppermute | solution.py:166
  7.4 7.0 %copy-start.23 = (bf16[1,32,1024]{2,1,0:T(8,128)(2,1)S(1)}, bf16[1,32,1024]{2,1,0:T(8,128)(2,1)}, u32[]{:S(2)}) copy-start(bf16[1,32,1024]{2,1,0:T(8,128)(2,1)} %param.10) | copy-start | bytes 196612
  7.5 7.0 %copy-start.24 = (bf16[1,32,1024]{2,1,0:T(8,128)(2,1)S(1)}, bf16[1,32,1024]{2,1,0:T(8,128)(2,1)}, u32[]{:S(2)}) copy-start(bf16[1,32,1024]{2,1,0:T(8,128)(2,1)} %param.11) | copy-start | bytes 196612
  7.5 58.0 %all-to-all-start = ((bf16[8,2,128,1024]{3,2,1,0:T(8,128)(2,1)}), bf16[8,2,128,1024]{3,2,1,0:T(8,128)(2,1)}, u32[]{:S(2)}, u32[]{:S(2)}) async-start(bf16[8,2,128,1024]{3,2,1,0:T(8,128)(2,1)} %shard_map.94), calls=%async_computation | async-start | bytes 8388608 | tf_op jit(solution)/shard_map/all_to_all | solution.py:185
  14.6 31.6 %copy-start.15 = (bf16[2,2,32,1024]{3,2,1,0:T(8,128)(2,1)}, bf16[2,2,32,1024]{3,2,1,0:T(8,128)(2,1)S(1)}, u32[]{:S(2)}) copy-start(bf16[2,2,32,1024]{3,2,1,0:T(8,128)(2,1)S(1)} %pad_maximum_fusion.refs_0_) | copy-start | bytes 786436
  14.6 10.9 %collective-permute-start.2 = (bf16[2,2,32,1024]{3,2,1,0:T(8,128)(2,1)S(1)}, bf16[2,2,32,1024]{3,2,1,0:T(8,128)(2,1)S(1)}, u32[]{:S(2)}, u32[]{:S(2)}) collective-permute-start(bf16[2,2,32,1024]{3,2,1,0:T(8,128)(2,1)S(1)} %pad_maximum_fusion.refs_0_), channel_id=1, source_target_pairs={{0,32},{32,64},{64,96},{96,128},{128,160},{160,192},{192,224},{224... | collective-permute-start | bytes 786440 | tf_op jit(solution)/shard_map/ppermute | solution.py:179
  16.3 9.2 %collective-permute-start.6 = (bf16[2,2,32,1024]{3,2,1,0:T(8,128)(2,1)S(1)}, bf16[2,2,32,1024]{3,2,1,0:T(8,128)(2,1)S(1)}, u32[]{:S(2)}, u32[]{:S(2)}) collective-permute-start(bf16[2,2,32,1024]{3,2,1,0:T(8,128)(2,1)S(1)} %pad_maximum_fusion.refs_0_), channel_id=1, source_target_pairs={{0,224},{32,0},{64,32},{96,64},{128,96},{160,128},{192,160},{224,1... | collective-permute-start | bytes 786440 | tf_op jit(solution)/shard_map/ppermute | solution.py:181
  25.4 20.7 %copy-start.16 = (bf16[2,2,32,1024]{3,2,1,0:T(8,128)(2,1)}, bf16[2,2,32,1024]{3,2,1,0:T(8,128)(2,1)S(1)}, u32[]{:S(2)}) copy-start(bf16[2,2,32,1024]{3,2,1,0:T(8,128)(2,1)S(1)} %collective-permute-done.2.refs_1_) | copy-start | bytes 786436
  25.4 7.1 %collective-permute-start.3 = (bf16[2,2,32,1024]{3,2,1,0:T(8,128)(2,1)S(1)}, bf16[2,2,32,1024]{3,2,1,0:T(8,128)(2,1)S(1)}, u32[]{:S(2)}, u32[]{:S(2)}) collective-permute-start(bf16[2,2,32,1024]{3,2,1,0:T(8,128)(2,1)S(1)} %collective-permute-done.2.refs_1_), channel_id=1, source_target_pairs={{0,32},{32,64},{64,96},{96,128},{128,160},{160,192},{192,224},{224... | collective-permute-start | bytes 786440 | tf_op jit(solution)/shard_map/ppermute | solution.py:179
  25.4 20.7 %copy-start.17 = (bf16[2,2,32,1024]{3,2,1,0:T(8,128)(2,1)}, bf16[2,2,32,1024]{3,2,1,0:T(8,128)(2,1)S(1)}, u32[]{:S(2)}) copy-start(bf16[2,2,32,1024]{3,2,1,0:T(8,128)(2,1)S(1)} %collective-permute-done.6.refs_7_) | copy-start | bytes 786436
  25.5 7.0 %collective-permute-start.7 = (bf16[2,2,32,1024]{3,2,1,0:T(8,128)(2,1)S(1)}, bf16[2,2,32,1024]{3,2,1,0:T(8,128)(2,1)S(1)}, u32[]{:S(2)}, u32[]{:S(2)}) collective-permute-start(bf16[2,2,32,1024]{3,2,1,0:T(8,128)(2,1)S(1)} %collective-permute-done.6.refs_7_), channel_id=1, source_target_pairs={{0,224},{32,0},{64,32},{96,64},{128,96},{160,128},{192,160},{224,1... | collective-permute-start | bytes 786440 | tf_op jit(solution)/shard_map/ppermute | solution.py:181
  32.5 13.7 %copy-start.18 = (bf16[2,2,32,1024]{3,2,1,0:T(8,128)(2,1)}, bf16[2,2,32,1024]{3,2,1,0:T(8,128)(2,1)S(1)}, u32[]{:S(2)}) copy-start(bf16[2,2,32,1024]{3,2,1,0:T(8,128)(2,1)S(1)} %collective-permute-done.3.refs_2_) | copy-start | bytes 786436
  32.5 6.8 %collective-permute-start.4 = (bf16[2,2,32,1024]{3,2,1,0:T(8,128)(2,1)S(1)}, bf16[2,2,32,1024]{3,2,1,0:T(8,128)(2,1)S(1)}, u32[]{:S(2)}, u32[]{:S(2)}) collective-permute-start(bf16[2,2,32,1024]{3,2,1,0:T(8,128)(2,1)S(1)} %collective-permute-done.3.refs_2_), channel_id=1, source_target_pairs={{0,32},{32,64},{64,96},{96,128},{128,160},{160,192},{192,224},{224... | collective-permute-start | bytes 786440 | tf_op jit(solution)/shard_map/ppermute | solution.py:179
  32.5 13.7 %copy-start.19 = (bf16[2,2,32,1024]{3,2,1,0:T(8,128)(2,1)}, bf16[2,2,32,1024]{3,2,1,0:T(8,128)(2,1)S(1)}, u32[]{:S(2)}) copy-start(bf16[2,2,32,1024]{3,2,1,0:T(8,128)(2,1)S(1)} %collective-permute-done.7.refs_6_) | copy-start | bytes 786436
  32.5 7.4 %collective-permute-start.8 = (bf16[2,2,32,1024]{3,2,1,0:T(8,128)(2,1)S(1)}, bf16[2,2,32,1024]{3,2,1,0:T(8,128)(2,1)S(1)}, u32[]{:S(2)}, u32[]{:S(2)}) collective-permute-start(bf16[2,2,32,1024]{3,2,1,0:T(8,128)(2,1)S(1)} %collective-permute-done.7.refs_6_), channel_id=1, source_target_pairs={{0,224},{32,0},{64,32},{96,64},{128,96},{160,128},{192,160},{224,1... | collective-permute-start | bytes 786440 | tf_op jit(solution)/shard_map/ppermute | solution.py:181
  39.3 6.9 %copy-start.20 = (bf16[2,2,32,1024]{3,2,1,0:T(8,128)(2,1)}, bf16[2,2,32,1024]{3,2,1,0:T(8,128)(2,1)S(1)}, u32[]{:S(2)}) copy-start(bf16[2,2,32,1024]{3,2,1,0:T(8,128)(2,1)S(1)} %collective-permute-done.4.refs_3_) | copy-start | bytes 786436
  39.3 6.8 %collective-permute-start.5 = (bf16[2,2,32,1024]{3,2,1,0:T(8,128)(2,1)S(1)}, bf16[2,2,32,1024]{3,2,1,0:T(8,128)(2,1)S(1)}, u32[]{:S(2)}, u32[]{:S(2)}) collective-permute-start(bf16[2,2,32,1024]{3,2,1,0:T(8,128)(2,1)S(1)} %collective-permute-done.4.refs_3_), channel_id=1, source_target_pairs={{0,32},{32,64},{64,96},{96,128},{128,160},{160,192},{192,224},{224... | collective-permute-start | bytes 786440 | tf_op jit(solution)/shard_map/ppermute | solution.py:179
  39.9 6.3 %copy-start.21 = (bf16[2,2,32,1024]{3,2,1,0:T(8,128)(2,1)}, bf16[2,2,32,1024]{3,2,1,0:T(8,128)(2,1)S(1)}, u32[]{:S(2)}) copy-start(bf16[2,2,32,1024]{3,2,1,0:T(8,128)(2,1)S(1)} %collective-permute-done.8.refs_5_) | copy-start | bytes 786436
  50.5 8.5 %collective-permute-start.9 = (bf16[8,2,2,32,1024]{4,3,2,1,0:T(8,128)(2,1)}, bf16[8,2,2,32,1024]{4,3,2,1,0:T(8,128)(2,1)S(1)}, u32[]{:S(2)}, u32[]{:S(2)}) collective-permute-start(bf16[8,2,2,32,1024]{4,3,2,1,0:T(8,128)(2,1)} %shard_map.95.mine), channel_id=1, source_target_pairs={{0,8},{8,0},{1,9},{9,1},{2,10},{10,2},{3,11},{11,3},{4,12},{12,4},... | collective-permute-start | bytes 6291464 | tf_op jit(solution)/shard_map/ppermute | solution.py:166
  60.4 1.6 copy-start.1
  62.0 1.6 copy-start.4
  65.5 2.9 %copy-start.7 = (bf16[8,2,2,32,1024]{4,3,2,1,0:T(8,128)(2,1)S(1)}, bf16[8,2,2,32,1024]{4,3,2,1,0:T(8,128)(2,1)}, u32[]{:S(2)}) copy-start(bf16[8,2,2,32,1024]{4,3,2,1,0:T(8,128)(2,1)} %copy-done.6) | copy-start | bytes 6291460
  68.4 2.4 %copy-start.13 = (bf16[8,1,128,1024]{3,2,1,0:T(8,128)(2,1)}, bf16[8,1,128,1024]{3,2,1,0:T(8,128)(2,1)S(1)}, u32[]{:S(2)}) copy-start(bf16[8,1,128,1024]{3,2,1,0:T(8,128)(2,1)S(1)} %get-tuple-element.30) | copy-start | bytes 6291460
  68.4 2.4 %copy-start.8 = (bf16[8,1,128,1024]{3,2,1,0:T(8,128)(2,1)}, bf16[8,1,128,1024]{3,2,1,0:T(8,128)(2,1)S(1)}, u32[]{:S(2)}) copy-start(bf16[8,1,128,1024]{3,2,1,0:T(8,128)(2,1)S(1)} %get-tuple-element.29) | copy-start | bytes 6291460
  72.1 3.8 %collective-permute-start.10 = (bf16[512,1024]{1,0:T(8,128)(2,1)S(1)}, bf16[512,1024]{1,0:T(8,128)(2,1)}, u32[]{:S(2)}, u32[]{:S(2)}) collective-permute-start(bf16[512,1024]{1,0:T(8,128)(2,1)S(1)} %convolution_convert_fusion.1), channel_id=1, source_target_pairs={{0,8},{8,0},{1,9},{9,1},{2,10},{10,2},{3,11},{11,3},{4,12},{12,4},... | collective-permute-start | bytes 3145736 | tf_op jit(solution)/shard_map/ppermute | solution.py:166
  78.5 32.0 %all-to-all-start.1 = ((bf16[16,32,1024]{2,1,0:T(8,128)(2,1)}), bf16[16,32,1024]{2,1,0:T(8,128)(2,1)S(1)}, u32[]{:S(2)}, u32[]{:S(2)}) async-start(bf16[16,32,1024]{2,1,0:T(8,128)(2,1)} %bitcast.87), calls=%async_computation.1 | async-start | bytes 2097152 | tf_op jit(solution)/shard_map/all_to_all | solution.py:216
  89.9 5.5 %copy-start.9 = (f32[1024,1024]{1,0:T(8,128)}, f32[1024,1024]{1,0:T(8,128)S(1)}, u32[]{:S(2)}) copy-start(f32[1024,1024]{1,0:T(8,128)S(1)} %convolution_multiply_fusion) | copy-start | bytes 12582916
  89.9 3.1 %copy-start.14 = (bf16[8,1,128,1024]{3,2,1,0:T(8,128)(2,1)S(1)}, bf16[8,1,128,1024]{3,2,1,0:T(8,128)(2,1)}, u32[]{:S(2)}) copy-start(bf16[8,1,128,1024]{3,2,1,0:T(8,128)(2,1)} %copy-done.13) | copy-start | bytes 6291460
  91.0 7.8 %collective-permute-start.12 = (bf16[8,2,32,1024]{3,2,1,0:T(8,128)(2,1)}, bf16[8,2,32,1024]{3,2,1,0:T(8,128)(2,1)}, u32[]{:S(2)}, u32[]{:S(2)}) collective-permute-start(bf16[8,2,32,1024]{3,2,1,0:T(8,128)(2,1)} %fusion.3), channel_id=1, source_target_pairs={{0,8},{8,0},{1,9},{9,1},{2,10},{10,2},{3,11},{11,3},{4,12},{12,4},... | collective-permute-start | bytes 3145736 | tf_op jit(solution)/shard_map/ppermute | solution.py:166
  95.4 2.0 %copy-start.10 = (f32[1024,1024]{1,0:T(8,128)}, f32[1024,1024]{1,0:T(8,128)S(1)}, u32[]{:S(2)}) copy-start(f32[1024,1024]{1,0:T(8,128)S(1)} %fusion.21) | copy-start | bytes 12582916
  98.6 3.0 %collective-permute-start.11 = (bf16[8,2,32,1024]{3,2,1,0:T(8,128)(2,1)}, bf16[8,2,32,1024]{3,2,1,0:T(8,128)(2,1)}, u32[]{:S(2)}, u32[]{:S(2)}) collective-permute-start(bf16[8,2,32,1024]{3,2,1,0:T(8,128)(2,1)} %fusion.2), channel_id=1, source_target_pairs={{0,8},{8,0},{1,9},{9,1},{2,10},{10,2},{3,11},{11,3},{4,12},{12,4},... | collective-permute-start | bytes 3145736 | tf_op jit(solution)/shard_map/ppermute | solution.py:166
  98.9 3.1 %copy-start.11 = (f32[1024,1024]{1,0:T(8,128)S(1)}, f32[1024,1024]{1,0:T(8,128)}, u32[]{:S(2)}) copy-start(f32[1024,1024]{1,0:T(8,128)} %copy-done.10) | copy-start | bytes 12582916
  105.1 26.7 %collective-permute-start.13 = (bf16[8,64,1024]{2,1,0:T(8,128)(2,1)}, bf16[8,64,1024]{2,1,0:T(8,128)(2,1)}, u32[]{:S(2)}, u32[]{:S(2)}) collective-permute-start(bf16[8,64,1024]{2,1,0:T(8,128)(2,1)} %get-tuple-element.32), channel_id=1, source_target_pairs={{0,16},{16,0},{1,17},{17,1},{2,18},{18,2},{3,19},{19,3},{4,20},{20... | collective-permute-start | bytes 3145736 | tf_op jit(solution)/shard_map/ppermute | solution.py:166
  111.4 23.5 %all-to-all-start.2 = ((bf16[8,32,1024]{2,1,0:T(8,128)(2,1)}), bf16[8,32,1024]{2,1,0:T(8,128)(2,1)S(1)}, u32[]{:S(2)}, u32[]{:S(2)}) async-start(bf16[8,32,1024]{2,1,0:T(8,128)(2,1)} %copy-done.2), calls=%async_computation.2 | async-start | bytes 1048576 | tf_op jit(solution)/shard_map/all_to_all | solution.py:217
  117.0 24.8 %copy-start.5 = (f32[1,1024]{1,0:T(1,128)S(1)}, f32[1,1024]{1,0:T(1,128)}, u32[]{:S(2)}) copy-start(f32[1,1024]{1,0:T(1,128)} %eig_cols.1) | copy-start | bytes 12292
  134.9 35.1 %all-to-all-start.3 = ((bf16[8,64,1024]{2,1,0:T(8,128)(2,1)}), bf16[8,64,1024]{2,1,0:T(8,128)(2,1)}, u32[]{:S(2)}, u32[]{:S(2)}) async-start(bf16[8,64,1024]{2,1,0:T(8,128)(2,1)} %add_convert_fusion), calls=%async_computation.3 | async-start | bytes 2097152 | tf_op jit(solution)/shard_map/all_to_all | solution.py:235
  141.8 14.2 %copy-start.25 = (s32[8]{0:T(128)S(1)}, s32[8]{0:T(128)}, u32[]{:S(2)}) copy-start(s32[8]{0:T(128)} %assign.1) | copy-start | bytes 100
  143.2 2.0 %collective-permute-start.14 = (f32[64,1024]{1,0:T(8,128)S(1)}, f32[64,1024]{1,0:T(8,128)S(1)}, u32[]{:S(2)}, u32[]{:S(2)}) collective-permute-start(f32[64,1024]{1,0:T(8,128)S(1)} %dynamic-slice_bitcast_fusion), channel_id=1, source_target_pairs={{0,8},{8,0},{1,9},{9,1},{2,10},{10,2},{3,11},{11,3},{4,12},{12,4},... | collective-permute-start | bytes 786440 | tf_op jit(solution)/shard_map/ppermute | solution.py:166
  145.3 4.9 %collective-permute-start.15 = (f32[32,1024]{1,0:T(8,128)S(1)}, f32[32,1024]{1,0:T(8,128)S(1)}, u32[]{:S(2)}, u32[]{:S(2)}) collective-permute-start(f32[32,1024]{1,0:T(8,128)S(1)} %dynamic-slice_bitcast_fusion.1), channel_id=1, source_target_pairs={{0,16},{16,0},{1,17},{17,1},{2,18},{18,2},{3,19},{19,3},{4,20},{20... | collective-permute-start | bytes 393224 | tf_op jit(solution)/shard_map/ppermute | solution.py:166
  150.3 11.2 %collective-permute-start.16 = (bf16[32,1024]{1,0:T(8,128)(2,1)S(1)}, bf16[32,1024]{1,0:T(8,128)(2,1)S(1)}, u32[]{:S(2)}, u32[]{:S(2)}) collective-permute-start(bf16[32,1024]{1,0:T(8,128)(2,1)S(1)} %fusion.10), channel_id=1, source_target_pairs={{0,7},{1,4},{2,5},{3,6},{4,3},{5,0},{6,1},{7,2},{8,15},{9,12},{10,... | collective-permute-start | bytes 196616 | tf_op jit(solution)/shard_map/ppermute | solution.py:248
  154.6 8.4 %collective-permute-start.17 = (bf16[32,1024]{1,0:T(8,128)(2,1)S(1)}, bf16[32,1024]{1,0:T(8,128)(2,1)S(1)}, u32[]{:S(2)}, u32[]{:S(2)}) collective-permute-start(bf16[32,1024]{1,0:T(8,128)(2,1)S(1)} %fusion.10), channel_id=1, source_target_pairs={{0,6},{1,7},{2,4},{3,5},{4,2},{5,3},{6,0},{7,1},{8,14},{9,15},{10,... | collective-permute-start | bytes 196616 | tf_op jit(solution)/shard_map/ppermute | solution.py:248
  156.0 7.7 %collective-permute-start.18 = (bf16[32,1024]{1,0:T(8,128)(2,1)S(1)}, bf16[32,1024]{1,0:T(8,128)(2,1)S(1)}, u32[]{:S(2)}, u32[]{:S(2)}) collective-permute-start(bf16[32,1024]{1,0:T(8,128)(2,1)S(1)} %fusion.10), channel_id=1, source_target_pairs={{0,5},{1,6},{2,7},{3,4},{4,1},{5,2},{6,3},{7,0},{8,13},{9,14},{10,... | collective-permute-start | bytes 196616 | tf_op jit(solution)/shard_map/ppermute | solution.py:248
  158.2 5.5 %collective-permute-start.19 = (bf16[32,1024]{1,0:T(8,128)(2,1)S(1)}, bf16[32,1024]{1,0:T(8,128)(2,1)S(1)}, u32[]{:S(2)}, u32[]{:S(2)}) collective-permute-start(bf16[32,1024]{1,0:T(8,128)(2,1)S(1)} %fusion.10), channel_id=1, source_target_pairs={{0,4},{1,5},{2,6},{3,7},{4,0},{5,1},{6,2},{7,3},{8,12},{9,13},{10,... | collective-permute-start | bytes 196616 | tf_op jit(solution)/shard_map/ppermute | solution.py:248
  159.3 4.4 %collective-permute-start.20 = (bf16[32,1024]{1,0:T(8,128)(2,1)S(1)}, bf16[32,1024]{1,0:T(8,128)(2,1)S(1)}, u32[]{:S(2)}, u32[]{:S(2)}) collective-permute-start(bf16[32,1024]{1,0:T(8,128)(2,1)S(1)} %fusion.10), channel_id=1, source_target_pairs={{0,3},{1,0},{2,1},{3,2},{4,7},{5,4},{6,5},{7,6},{8,11},{9,8},{10,9... | collective-permute-start | bytes 196616 | tf_op jit(solution)/shard_map/ppermute | solution.py:248
  161.4 5.0 %collective-permute-start.21 = (bf16[32,1024]{1,0:T(8,128)(2,1)S(1)}, bf16[32,1024]{1,0:T(8,128)(2,1)S(1)}, u32[]{:S(2)}, u32[]{:S(2)}) collective-permute-start(bf16[32,1024]{1,0:T(8,128)(2,1)S(1)} %fusion.10), channel_id=1, source_target_pairs={{0,2},{1,3},{2,0},{3,1},{4,6},{5,7},{6,4},{7,5},{8,10},{9,11},{10,... | collective-permute-start | bytes 196616 | tf_op jit(solution)/shard_map/ppermute | solution.py:248
  162.9 4.7 %collective-permute-start.22 = (bf16[32,1024]{1,0:T(8,128)(2,1)S(1)}, bf16[32,1024]{1,0:T(8,128)(2,1)S(1)}, u32[]{:S(2)}, u32[]{:S(2)}) collective-permute-start(bf16[32,1024]{1,0:T(8,128)(2,1)S(1)} %fusion.10), channel_id=1, source_target_pairs={{0,1},{1,2},{2,3},{3,0},{4,5},{5,6},{6,7},{7,4},{8,9},{9,10},{10,1... | collective-permute-start | bytes 196616 | tf_op jit(solution)/shard_map/ppermute | solution.py:248
  (5 other events, 5.6 us)
